TPU v7x, 32 devices: a whole 2x2x4 slice. The times are simulated.
32 devices in a mesh: dp: 2 (over x), ty: 4 (over y, core), tx: 4 (over z).
Axes of the slice: x: 2, y: 2, z: 4, core: 2. Of those that a mesh axis runs over, the one named last changes fastest.
Arguments:
- image_in: bfloat16 [2, 64, 64, 768], P('dp', 'ty', 'tx'), may hold values from -6 to 6
- params: float32 [7090560], P(('dp', 'ty', 'tx')), may hold values from -1.2124356 to 1.4, as said below
- cotangent: bfloat16 [2, 64, 64, 768], P('dp', 'ty', 'tx'), may hold values from -6 to 6
Outputs:
- image_out: bfloat16 [2, 64, 64, 768], P('dp', 'ty', 'tx')
- grad_image: bfloat16 [2, 64, 64, 768], P('dp', 'ty', 'tx')
- grad_params: float32 [7090560], P(('dp', 'ty', 'tx'))
Inputs may be any that keep to these rules, and one draw needn't show every extreme that they name: params holds the block's parameters in the order of the first step; entries past 7090560 are unused.
All inputs are finite; a program needn't handle non-finite values.
Results may differ from a plain program's by a relative error of at most 0.018.
Values may be sent and summed in bfloat16 or wider, within the bound.
A program may use at most 320 MiB of HBM per device.

v0:
```python
import math

import jax
import jax.numpy as jnp
from jax import lax
from jax.sharding import PartitionSpec as P

D = 768
HEADS = 12
HEAD_DIM = 64
MLP = 3072
WIN = 14


highest = lax.Precision.HIGHEST
epsilon = 1e-06


def from_behind(array, axis, by):
    size = lax.axis_size(axis)
    pairs = [(i, i + by) for i in range(size) if 0 <= i + by < size]
    return lax.ppermute(array, axis, pairs)


def unpack(vector):
    layouts = (
        (D, 3 * D),
        (2 * D,),
        (2 * WIN - 1, HEAD_DIM),
        (2 * WIN - 1, HEAD_DIM),
        (D, D),
        (D,),
        (D,),
        (D,),
        (D,),
        (D,),
        (D, MLP),
        (MLP,),
        (MLP, D),
        (D,),
    )
    pieces = []
    offset = 0
    for layout in layouts:
        length = math.prod(layout)
        pieces.append(vector[offset : offset + length].reshape(layout))
        offset = offset + length
    return tuple(pieces)


def layer_norm(features_in, gain_vector, shift_vector):
    center = features_in - jnp.mean(features_in, axis=-1, keepdims=True)
    spread = jnp.mean(center * center, axis=-1, keepdims=True)
    return center * lax.rsqrt(spread + epsilon) * gain_vector + shift_vector


def relative_picker():
    places = jnp.arange(WIN, dtype=jnp.int32)
    target = (places[:, None] - places[None, :] + WIN - 1).reshape(WIN * WIN)
    return (target[:, None] == jnp.arange(2 * WIN - 1, dtype=jnp.int32)[None, :]).astype(
        jnp.bfloat16
    )


def looked_up(picker, lookup_table):
    return (
        jnp.dot(picker, lookup_table, preferred_element_type=jnp.float32)
        .astype(jnp.bfloat16)
        .reshape(WIN, WIN, HEAD_DIM)
    )


def window_offsets(tile_index, tile_count, tile_len):
    windows_side = (tile_len * tile_count + WIN - 1) // WIN
    first_window = (tile_len * tile_index + WIN - 1) // WIN
    window_ids = first_window + jnp.arange(2, dtype=jnp.int32)
    offsets = WIN * window_ids - tile_len * tile_index
    usable = (WIN * window_ids < tile_len * (tile_index + 1)) & (window_ids < windows_side)
    return (offsets, usable)


def cut_windows(extended, row_offsets, col_offsets):
    batch_size, features = (extended.shape[0], extended.shape[-1])
    anchor = jnp.zeros((), jnp.int32)
    collected = []
    for row_pick in range(2):
        for col_pick in range(2):
            starts = (anchor, row_offsets[row_pick], col_offsets[col_pick], anchor)
            window = lax.dynamic_slice(extended, starts, (batch_size, WIN, WIN, features))
            collected.append(window.reshape(batch_size, WIN * WIN, features))
    return jnp.stack(collected, axis=1)


def place_windows(windows, row_offsets, col_offsets, side_len):
    batch_size, features = (windows.shape[0], windows.shape[-1])
    anchor = jnp.zeros((), jnp.int32)
    canvas = jnp.zeros((batch_size, side_len, side_len, features), windows.dtype)
    for row_pick in range(2):
        for col_pick in range(2):
            starts = (anchor, row_offsets[row_pick], col_offsets[col_pick], anchor)
            current = lax.dynamic_slice(canvas, starts, (batch_size, WIN, WIN, features))
            update = windows[:, 2 * row_pick + col_pick].reshape(batch_size, WIN, WIN, features)
            canvas = lax.dynamic_update_slice(canvas, current + update, starts)
    return canvas


def scores_of(queries, window_keys, rel_h, rel_w):
    window_count = queries.shape[0]
    grid_queries = queries.reshape(window_count, WIN, WIN, HEADS, HEAD_DIM)
    keyed = window_keys.reshape(window_count, WIN * WIN, HEADS, HEAD_DIM)
    direct = jnp.einsum(
        "nyxhc,nkhc->nhyxk", grid_queries, keyed, preferred_element_type=jnp.float32
    ) * HEAD_DIM ** (-0.5)
    along_h = jnp.einsum(
        "nyxhc,ykc->nhyxk", grid_queries, rel_h, preferred_element_type=jnp.float32
    )
    along_w = jnp.einsum(
        "nyxhc,xkc->nhyxk", grid_queries, rel_w, preferred_element_type=jnp.float32
    )
    total = (
        direct.reshape(window_count, HEADS, WIN, WIN, WIN, WIN)
        + along_h[..., :, None]
        + along_w[..., None, :]
    )
    return total.reshape(window_count, HEADS, WIN * WIN, WIN * WIN)


def forward_image(queries, window_keys, window_values, rel_h, rel_w):
    window_count = queries.shape[0]
    scores = scores_of(queries, window_keys, rel_h, rel_w)
    highest_score = jnp.max(scores, axis=-1, keepdims=True)
    expanded = jnp.exp(scores - highest_score)
    total = jnp.sum(expanded, axis=-1, keepdims=True)
    softmaxed = (expanded / total).astype(jnp.bfloat16)
    valued = window_values.reshape(window_count, WIN * WIN, HEADS, HEAD_DIM)
    attended = jnp.einsum("nhqk,nkhc->nqhc", softmaxed, valued, preferred_element_type=jnp.float32)
    logsum = (highest_score + jnp.log(total))[..., 0]
    return (attended.reshape(window_count, WIN * WIN, D).astype(jnp.bfloat16), logsum)


def backward_image(queries, window_keys, window_values, logsum, grad_attended, rel_h, rel_w):
    window_count = queries.shape[0]
    tokens_win = WIN * WIN
    head_scale = HEAD_DIM ** (-0.5)
    scores = scores_of(queries, window_keys, rel_h, rel_w)
    probs_full = jnp.exp(scores - logsum[..., None])
    grad_heads = grad_attended.reshape(window_count, tokens_win, HEADS, HEAD_DIM)
    valued = window_values.reshape(window_count, tokens_win, HEADS, HEAD_DIM)
    keyed = window_keys.reshape(window_count, tokens_win, HEADS, HEAD_DIM)
    queried = queries.reshape(window_count, tokens_win, HEADS, HEAD_DIM)
    grad_probs = jnp.einsum(
        "nqhc,nkhc->nhqk", grad_heads, valued, preferred_element_type=jnp.float32
    )
    inner = jnp.sum(probs_full * grad_probs, axis=-1, keepdims=True)
    grad_scores = (probs_full * (grad_probs - inner)).astype(jnp.bfloat16)
    grad_queries = (
        jnp.einsum("nhqk,nkhc->nqhc", grad_scores, keyed, preferred_element_type=jnp.float32)
        * head_scale
    )
    grad_keys = (
        jnp.einsum("nhqk,nqhc->nkhc", grad_scores, queried, preferred_element_type=jnp.float32)
        * head_scale
    )
    grad_values = jnp.einsum(
        "nhqk,nqhc->nkhc",
        probs_full.astype(jnp.bfloat16),
        grad_heads,
        preferred_element_type=jnp.float32,
    )
    grid_scores = grad_scores.reshape(window_count, HEADS, WIN, WIN, WIN, WIN)
    grad_h = jnp.sum(grid_scores, axis=5, dtype=jnp.float32)
    grad_w = jnp.sum(grid_scores, axis=4, dtype=jnp.float32)
    query_wide = queries.astype(jnp.float32).reshape(window_count, WIN, WIN, HEADS, HEAD_DIM)
    extra_h = jnp.einsum("nhyxk,ykc->nyxhc", grad_h, rel_h.astype(jnp.float32), precision=highest)
    extra_w = jnp.einsum("nhyxk,xkc->nyxhc", grad_w, rel_w.astype(jnp.float32), precision=highest)
    grad_queries = grad_queries.reshape(window_count, WIN, WIN, HEADS, HEAD_DIM) + extra_h + extra_w
    table_grad_h = jnp.einsum("nhyxk,nyxhc->ykc", grad_h, query_wide, precision=highest)
    table_grad_w = jnp.einsum("nhyxk,nyxhc->xkc", grad_w, query_wide, precision=highest)
    return (
        grad_queries.reshape(window_count, tokens_win, D).astype(jnp.bfloat16),
        grad_keys.reshape(window_count, tokens_win, D).astype(jnp.bfloat16),
        grad_values.reshape(window_count, tokens_win, D).astype(jnp.bfloat16),
        table_grad_h,
        table_grad_w,
    )


def shards(image_in, params, cotangent):
    gathered = lax.all_gather(params.astype(jnp.bfloat16), ("dp", "ty", "tx"), axis=0, tiled=True)
    pieces = unpack(gathered)
    (
        w_qkv,
        qv_bias,
        table_h,
        table_w,
        w_proj,
        b_proj,
        gain_one,
        shift_one,
        gain_two,
        shift_two,
        w_up,
        b_up,
        w_down,
        b_down,
    ) = pieces
    images_here, tile_len = (image_in.shape[0], image_in.shape[1])
    rim = WIN - 1
    side_len = tile_len + rim
    tokens_win = WIN * WIN
    row_offsets, row_usable = window_offsets(lax.axis_index("ty"), lax.axis_size("ty"), tile_len)
    col_offsets, col_usable = window_offsets(lax.axis_index("tx"), lax.axis_size("tx"), tile_len)
    window_mask = (row_usable[:, None] & col_usable[None, :]).reshape(4)[None, :, None, None]
    picker = relative_picker()
    rel_h = looked_up(picker, table_h)
    rel_w = looked_up(picker, table_w)
    gain_one_wide, shift_one_wide = (gain_one.astype(jnp.float32), shift_one.astype(jnp.float32))
    gain_two_wide, shift_two_wide = (gain_two.astype(jnp.float32), shift_two.astype(jnp.float32))
    inputs = image_in.astype(jnp.float32)
    normed = layer_norm(inputs, gain_one_wide, shift_one_wide).astype(jnp.bfloat16)
    lower_rim = from_behind(normed[:, :rim], "ty", -1)
    taller = jnp.concatenate([normed, lower_rim], axis=1)
    beside = from_behind(taller[:, :, :rim], "tx", -1)
    extended = jnp.concatenate([taller, beside], axis=2)
    windows = cut_windows(extended, row_offsets, col_offsets)
    flat_rows = windows.reshape(-1, D)
    mixed_rows = jnp.dot(flat_rows, w_qkv, preferred_element_type=jnp.float32)
    window_shape = (images_here, 4, tokens_win, D)
    queries = (
        (mixed_rows[:, :D] + qv_bias[:D].astype(jnp.float32))
        .astype(jnp.bfloat16)
        .reshape(window_shape)
    )
    window_keys = mixed_rows[:, D : 2 * D].astype(jnp.bfloat16).reshape(window_shape)
    window_values = (
        (mixed_rows[:, 2 * D :] + qv_bias[D:].astype(jnp.float32))
        .astype(jnp.bfloat16)
        .reshape(window_shape)
    )
    attended, logsum = lax.map(
        lambda packed: forward_image(packed[0], packed[1], packed[2], rel_h, rel_w),
        (queries, window_keys, window_values),
    )
    projected = jnp.dot(
        attended.reshape(-1, D), w_proj, preferred_element_type=jnp.float32
    ) + b_proj.astype(jnp.float32)
    projected = projected.astype(jnp.bfloat16).reshape(window_shape)
    projected = jnp.where(window_mask, projected, jnp.zeros_like(projected))
    canvas = place_windows(projected, row_offsets, col_offsets, side_len)
    from_left = from_behind(canvas[:, :, tile_len:], "tx", 1)
    narrowed = canvas[:, :, :tile_len].at[:, :, :rim].add(from_left)
    from_above = from_behind(narrowed[:, tile_len:], "ty", 1)
    branch = narrowed[:, :tile_len].at[:, :rim].add(from_above)
    middle = inputs + branch.astype(jnp.float32)
    hidden = layer_norm(middle, gain_two_wide, shift_two_wide).astype(jnp.bfloat16)
    hidden_rows = hidden.reshape(-1, D)
    pre_gelu = jnp.dot(hidden_rows, w_up, preferred_element_type=jnp.float32) + b_up.astype(
        jnp.float32
    )
    activated, gelu_pull = jax.vjp(
        lambda value_in: jax.nn.gelu(value_in, approximate=False), pre_gelu
    )
    activated = activated.astype(jnp.bfloat16)
    projected_down = (
        jnp.dot(activated, w_down, preferred_element_type=jnp.float32) + b_down.astype(jnp.float32)
    ).astype(jnp.bfloat16)
    image_out = (middle + projected_down.reshape(middle.shape).astype(jnp.float32)).astype(
        jnp.bfloat16
    )
    w_qkv_back, w_proj_back, w_up_back, w_down_back = (w_qkv, w_proj, w_up, w_down)
    rel_h_back, rel_w_back = (rel_h, rel_w)
    cot_rows = cotangent.reshape(-1, D)
    grad_w_down = jnp.dot(activated.T, cot_rows, preferred_element_type=jnp.float32)
    grad_b_down = jnp.sum(cot_rows, axis=0, dtype=jnp.float32)
    grad_act = jnp.dot(cot_rows, w_down_back.T, preferred_element_type=jnp.float32)
    grad_up = gelu_pull(grad_act)[0].astype(jnp.bfloat16)
    grad_w_up = jnp.dot(hidden_rows.T, grad_up, preferred_element_type=jnp.float32)
    grad_b_up = jnp.sum(grad_up, axis=0, dtype=jnp.float32)
    grad_hidden = jnp.dot(grad_up, w_up_back.T, preferred_element_type=jnp.float32).reshape(
        middle.shape
    )
    norm_two_pull = jax.vjp(layer_norm, middle, gain_two_wide, shift_two_wide)[1]
    grad_middle_part, grad_gain_two, grad_shift_two = norm_two_pull(grad_hidden)
    grad_middle = cotangent.astype(jnp.float32) + grad_middle_part
    grad_branch = grad_middle.astype(jnp.bfloat16)
    lower_grad = from_behind(grad_branch[:, :rim], "ty", -1)
    taller_grad = jnp.concatenate([grad_branch, lower_grad], axis=1)
    beside_grad = from_behind(taller_grad[:, :, :rim], "tx", -1)
    extended_grad = jnp.concatenate([taller_grad, beside_grad], axis=2)
    grad_windows = cut_windows(extended_grad, row_offsets, col_offsets)
    grad_windows = jnp.where(window_mask, grad_windows, jnp.zeros_like(grad_windows))
    grad_rows = grad_windows.reshape(-1, D)
    grad_w_proj = jnp.dot(attended.reshape(-1, D).T, grad_rows, preferred_element_type=jnp.float32)
    grad_b_proj = jnp.sum(grad_rows, axis=0, dtype=jnp.float32)
    grad_attended = (
        jnp.dot(grad_rows, w_proj_back.T, preferred_element_type=jnp.float32)
        .astype(jnp.bfloat16)
        .reshape(window_shape)
    )
    grad_queries, grad_keys, grad_values, table_grad_h, table_grad_w = lax.map(
        lambda packed: backward_image(
            packed[0], packed[1], packed[2], packed[3], packed[4], rel_h_back, rel_w_back
        ),
        (queries, window_keys, window_values, logsum, grad_attended),
    )
    picker_wide = picker.astype(jnp.float32).T
    grad_table_h = jnp.dot(
        picker_wide, jnp.sum(table_grad_h, axis=0).reshape(WIN * WIN, HEAD_DIM), precision=highest
    )
    grad_table_w = jnp.dot(
        picker_wide, jnp.sum(table_grad_w, axis=0).reshape(WIN * WIN, HEAD_DIM), precision=highest
    )
    grad_mixed = jnp.concatenate([grad_queries, grad_keys, grad_values], axis=-1).reshape(-1, 3 * D)
    grad_w_qkv = jnp.dot(flat_rows.T, grad_mixed, preferred_element_type=jnp.float32)
    grad_qv_bias = jnp.concatenate(
        [
            jnp.sum(grad_queries.reshape(-1, D), axis=0, dtype=jnp.float32),
            jnp.sum(grad_values.reshape(-1, D), axis=0, dtype=jnp.float32),
        ]
    )
    grad_normed_windows = (
        jnp.dot(grad_mixed, w_qkv_back.T, preferred_element_type=jnp.float32)
        .astype(jnp.bfloat16)
        .reshape(window_shape)
    )
    grad_canvas = place_windows(grad_normed_windows, row_offsets, col_offsets, side_len)
    grad_left = from_behind(grad_canvas[:, :, tile_len:], "tx", 1)
    grad_narrowed = grad_canvas[:, :, :tile_len].at[:, :, :rim].add(grad_left)
    grad_above = from_behind(grad_narrowed[:, tile_len:], "ty", 1)
    grad_normed = grad_narrowed[:, :tile_len].at[:, :rim].add(grad_above)
    norm_one_pull = jax.vjp(layer_norm, inputs, gain_one_wide, shift_one_wide)[1]
    grad_input_part, grad_gain_one, grad_shift_one = norm_one_pull(grad_normed.astype(jnp.float32))
    grad_image = (grad_middle + grad_input_part).astype(jnp.bfloat16)
    devices_all = lax.axis_size("dp") * lax.axis_size("ty") * lax.axis_size("tx")
    total_len = params.shape[0] * devices_all
    gradients = [
        grad_w_qkv,
        grad_qv_bias,
        grad_table_h,
        grad_table_w,
        grad_w_proj,
        grad_b_proj,
        grad_gain_one,
        grad_shift_one,
        grad_gain_two,
        grad_shift_two,
        grad_w_up,
        grad_b_up,
        grad_w_down,
        grad_b_down,
    ]
    used_len = sum((member.size for member in gradients))
    members = [member.reshape(-1) for member in gradients]
    members.append(jnp.zeros((total_len - used_len,), jnp.float32))
    padded_grad = jnp.concatenate(members)
    data_summed = lax.psum_scatter(
        padded_grad.astype(jnp.bfloat16), "dp", scatter_dimension=0, tiled=True
    )
    grad_params = lax.psum_scatter(
        data_summed, ("ty", "tx"), scatter_dimension=0, tiled=True
    ).astype(jnp.float32)
    return (image_out, grad_image, grad_params)


def solution(mesh):
    return jax.shard_map(
        shards,
        mesh=mesh,
        in_specs=(P("dp", "ty", "tx", None), P(("dp", "ty", "tx")), P("dp", "ty", "tx", None)),
        out_specs=(P("dp", "ty", "tx", None), P("dp", "ty", "tx", None), P(("dp", "ty", "tx"))),
        check_vma=False,
    )
```

profile of v0, /device:TPU:0, one launch (start us, length us, event | category | flops | bytes accessed | tf_op | source)
XLA Modules:
  0.0 1886.3 jit_solution(16842204750005846594)
XLA Ops:
  8.4 5.2 broadcast.404
  13.6 7.6 dynamic-update-slice.12
  28.0 245.7 %all-reduce.7.cloned.1.call-done = bf16[7090560]{0:T(1024)(128)(2,1)} async-done(((bf16[7090560]{0:T(1024)(128)(2,1)}), bf16[7090560]{0:T(1024)(128)(2,1)}) %all-reduce.7.cloned.1.call-update) | async-done | bytes 14181136
  291.0 5.2 reshape.802
  327.5 8.9 fusion.37
  336.4 8.4 copy.174
  344.8 27.3 %add.342 = f32[4,12,14,14,14,14]{5,4,0,3,2,1:T(8,128)} broadcast(f32[4,12,14,14,14]{4,0,3,2,1:T(4,128)} %copy.174), dimensions={0,1,2,3,4} | broadcast | bytes 7902720 | tf_op jit(solution)/shard_map/while/body/eval_jaxpr/add | solution.py:121
  372.1 54.7 %add.348 = f32[4,12,14,14,196]{4,0,3,2,1:T(4,128)} reshape(f32[4,12,14,14,14,14]{5,4,0,3,2,1:T(8,128)} %add.342) | data formatting | bytes 14751744 | tf_op jit(solution)/shard_map/while/body/eval_jaxpr/add | solution.py:121
  426.8 54.4 %reshape.843 = f32[4,12,196,196]{3,0,2,1:T(4,128)} reshape(f32[4,12,14,14,14,14]{5,4,0,3,2,1:T(8,128)} %add.342) | data formatting | bytes 14751744 | tf_op jit(solution)/shard_map/while/body/eval_jaxpr/add | solution.py:121
  481.3 8.9 fusion.40
  490.2 8.5 copy.180
  498.7 25.9 %add.345 = f32[4,12,14,14,14,14]{5,4,0,3,2,1:T(8,128)} broadcast(f32[4,12,14,14,14]{4,0,3,2,1:T(4,128)} %copy.180), dimensions={0,1,2,3,5} | broadcast | bytes 7902720 | tf_op jit(solution)/shard_map/while/body/eval_jaxpr/add | solution.py:121
  524.6 54.4 %add.350 = f32[4,12,14,14,196]{4,0,3,2,1:T(4,128)} reshape(f32[4,12,14,14,14,14]{5,4,0,3,2,1:T(8,128)} %add.345) | data formatting | bytes 14751744 | tf_op jit(solution)/shard_map/while/body/eval_jaxpr/add | solution.py:121
  579.0 54.4 %reshape.845 = f32[4,12,196,196]{3,0,2,1:T(4,128)} reshape(f32[4,12,14,14,14,14]{5,4,0,3,2,1:T(8,128)} %add.345) | data formatting | bytes 14751744 | tf_op jit(solution)/shard_map/while/body/eval_jaxpr/add | solution.py:121
  635.9 4.9 reshape.805
  640.8 27.4 %fusion.109 = (f32[4,12,14,14]{3,2,1,0:T(8,128)}, f32[4,12,14,14,196]{4,3,2,1,0:T(8,128)}) fusion(f32[4,12,14,14,196]{4,0,3,2,1:T(4,128)} %add.350, f32[4,12,14,14,196]{4,0,3,2,1:T(4,128)} %add.348, bf16[4,196,12,64,1]{1,0,3,2,4:T(4,128)(2,1)} %bitcast.121, bf16[4,14,14,12,64]{4,3,2,1,0:T(8,128)(2,1)S(1)} %reshape.804), kind=kOutput, calls=%fused_computation.197 | convolution fusion | flops 243394368 | bytes 24573696 | tf_op jit(solution)/shard_map/while/body/eval_jaxpr/nyxhc,nkhc->nhyxk/dot_general | solution.py:111
  668.2 17.5 copy.171
  685.7 16.9 exponential_reduce_fusion
  709.8 13.0 copy.177
  722.8 13.0 copy.182
  736.0 13.0 copy.176
  749.0 10.5 add_add_fusion
  771.9 5.7 dynamic_update_slice.41
  777.8 4.5 dynamic_update_slice.42
  782.5 4.9 dynamic_update_slice.43
  793.2 13.3 collective-permute-done.2
  806.9 5.4 scatter-add.14
  815.7 9.2 fusion.113
  824.8 9.2 reshape.815
  834.1 8.3 reshape.814
  844.0 9.5 multiply_convert_fusion.2
  875.9 9.4 reshape.831
  904.2 7.4 fusion.120
  911.6 7.4 multiply_reduce_fusion
  919.0 11.3 multiply_convert_fusion
  930.3 4.9 multiply_bitcast_fusion
  935.2 8.6 copy.203
  943.8 4.5 copy.202
  948.2 43.0 %reshape.833 = f32[4,12,14,14,14,14]{5,4,3,2,1,0:T(8,128)} reshape(f32[4,12,196,196]{3,2,1,0:T(8,128)} %copy.203) | data formatting | bytes 14751744 | tf_op jit(solution)/shard_map/while/body/eval_jaxpr/convert_element_type | solution.py:171
  991.3 30.5 %fusion.110 = (f32[4,12,14,14,14]{4,3,2,1,0:T(8,128)}, f32[4,12,14,14,14]{4,3,2,1,0:T(8,128)}) fusion(f32[4,12,14,14,14,14]{5,4,3,2,1,0:T(8,128)} %reshape.833), kind=kLoop, calls=%fused_computation.198 | loop fusion | flops 3424512 | bytes 8429568 | tf_op jit(solution)/shard_map/while/body/eval_jaxpr/reduce_sum | solution.py:171
  1021.8 7.9 fusion.68
  1033.8 9.1 fusion.119
  1045.3 5.1 convert_element_type.273
  1050.4 4.8 convert_element_type.284
  1057.7 5.4 copy.248
  1063.1 5.1 reshape.850
  1068.1 6.3 multiply_convert_fusion.1
  1076.9 5.4 copy.247
  1082.3 5.1 reshape.849
  1087.3 7.1 fusion.58
  1106.9 4.8 dynamic_update_slice.45
  1113.7 4.7 dynamic_update_slice.46
  1120.4 4.7 dynamic_update_slice.47
  1127.0 4.6 dynamic_update_slice.48
  1133.8 5.6 collective-permute-start.6
  1139.4 8.1 bitcast_convert_fusion
  1150.8 10.6 fusion.73
  1162.9 6.3 scatter-add.16
  1170.2 6.8 collective-permute-start.7
  1180.6 7.8 reshape.824
  1190.5 205.5 %concatenate.47 = bf16[7090560]{0:T(1024)(128)(2,1)} concatenate(bf16[1769472]{0:T(1024)(128)(2,1)} %reshape.824, bf16[768]{0:T(1024)(128)(2,1)S(1)} %reduce_sum.223, bf16[768]{0:T(1024)(128)(2,1)S(1)} %reduce_sum.228, bf16[1728]{0:T(1024)(128)(2,1)S(1)} %reshape.826, bf16[1728]{0:T(1024)(128)(2,1)S(1)} %reshape.828, bf16[589824]{0:T(1024)(128)(2,1)S(1)} %reshape.829, ...), dimensions={0} | concatenate | bytes 28362240 | tf_op jit(solution)/shard_map/concatenate | solution.py:355
  1397.9 318.5 %all-reduce.9.cloned.1.call-done = bf16[7090560]{0:T(1024)(128)(2,1)} async-done(((bf16[7090560]{0:T(1024)(128)(2,1)}), bf16[7090560]{0:T(1024)(128)(2,1)}) %all-reduce.9.cloned.1.call-update) | async-done | bytes 14181136
  1716.4 8.2 dynamic-slice.33
  1727.7 149.7 %all-reduce.11.cloned.1.call-done = bf16[3545280]{0:T(1024)(128)(2,1)} async-done(((bf16[3545280]{0:T(1024)(128)(2,1)}), bf16[3545280]{0:T(1024)(128)(2,1)}) %all-reduce.11.cloned.1.call-update) | async-done | bytes 7090576
  (319 shorter events, 172.6 us)
Async XLA Ops:
  7.2 266.6 %all-reduce.7.cloned.1.call-start = ((), (), s32[]{:S(2)}) async-start(), calls=%async_computation | async-start | bytes 28364800
  21.2 6.4 copy-start.4
  21.2 1695.2 %all-reduce.9.cloned.1.call-start = ((), (), s32[]{:S(2)}) async-start(), calls=%async_computation.1 | async-start | bytes 28364800
  27.7 247.4 %copy-start.38 = (f32[16,16]{1,0:T(8,128)}, f32[16,16]{1,0:T(8,128)S(1)}, u32[]{:S(2)}) copy-start(f32[16,16]{1,0:T(8,128)S(1)} %broadcast_multiply_fusion.2) | copy-start | bytes 3076
  27.9 247.2 %copy-start.47 = (f32[16,16]{1,0:T(8,128)}, f32[16,16]{1,0:T(8,128)S(1)}, u32[]{:S(2)}) copy-start(f32[16,16]{1,0:T(8,128)S(1)} %fusion.83) | copy-start | bytes 3076
  28.0 247.2 %copy-start.41 = (f32[16,16]{1,0:T(8,128)}, f32[16,16]{1,0:T(8,128)S(1)}, u32[]{:S(2)}) copy-start(f32[16,16]{1,0:T(8,128)S(1)} %fusion.101) | copy-start | bytes 3076
  275.4 11.6 copy-start.19
  275.4 4.6 collective-permute-start
  277.5 9.5 copy-start.53
  280.0 7.0 copy-start.30
  281.1 16.7 collective-permute-start.1
  303.7 12.8 copy-start.22
  323.7 3.8 copy-start.35
  327.5 313.3 %copy-start.1 = (bf16[4,14,14,12,64]{4,3,2,1,0:T(8,128)(2,1)}, bf16[4,14,14,12,64]{4,3,2,1,0:T(8,128)(2,1)S(1)}, u32[]{:S(2)}) copy-start(bf16[4,14,14,12,64]{4,3,2,1,0:T(8,128)(2,1)S(1)} %reshape.804) | copy-start | bytes 3612676
  426.8 54.4 %copy-start.33 = (bf16[14,14,64,1,1]{2,1,0,3,4:T(8,128)(2,1)S(1)}, bf16[14,14,64,1,1]{2,1,0,3,4:T(8,128)(2,1)}, u32[]{:S(2)}) copy-start(bf16[14,14,64,1,1]{2,1,0,3,4:T(8,128)(2,1)} %reshape.838) | copy-start | bytes 75268
  668.2 17.5 copy-start.21
  722.8 13.0 copy-start.25
  736.0 23.5 %copy-start.40 = (f32[4,12,196]{2,1,0:T(8,128)}, f32[4,12,196]{2,1,0:T(8,128)S(1)}, u32[]{:S(2)}) copy-start(f32[4,12,196]{2,1,0:T(8,128)S(1)} %reshape.847) | copy-start | bytes 112900
  749.0 10.5 copy-start.17
  759.5 3.8 copy-start
  765.8 3.9 copy-start.28
  765.8 5.3 copy-start.62
  791.8 14.7 collective-permute-start.2
  812.3 30.8 %collective-permute-start.3 = (bf16[1,13,16,768]{3,2,1,0:T(8,128)(2,1)S(1)}, bf16[1,13,16,768]{3,2,1,0:T(8,128)(2,1)S(1)}, u32[]{:S(2)}, u32[]{:S(2)}) collective-permute-start(bf16[1,13,16,768]{3,2,1,0:T(8,128)(2,1)S(1)} %slice.362), channel_id=1, source_target_pairs={{0,4},{4,8},{8,12},{1,5},{5,9},{9,13},{2,6},{6,10},{10,14},{3,7},{... | collective-permute-start | bytes 958472 | tf_op jit(solution)/shard_map/ppermute | solution.py:22
  834.1 9.1 copy-start.5
  843.7 9.8 slice-start.3
  843.7 12.6 slice-start.5
  843.9 9.6 copy-start.15
  843.9 9.6 slice-start.4
  844.0 12.3 slice-start.6
  853.5 5.7 copy-start.23
  856.3 2.9 copy-start.59
  860.6 4.7 copy-start.14
  861.7 6.7 copy-start.12
  863.3 6.1 collective-permute-start.4
  868.4 3.9 copy-start.24
  870.5 19.7 %collective-permute-start.5 = (bf16[1,29,13,768]{3,1,2,0:T(8,128)(2,1)}, bf16[1,29,13,768]{3,1,2,0:T(8,128)(2,1)}, u32[]{:S(2)}, u32[]{:S(2)}) collective-permute-start(bf16[1,29,13,768]{3,1,2,0:T(8,128)(2,1)} %copy.195), channel_id=1, source_target_pairs={{1,0},{2,1},{3,2},{5,4},{6,5},{7,6},{9,8},{10,9},{11,10},{13,12},{... | collective-permute-start | bytes 1737224 | tf_op jit(solution)/shard_map/ppermute | solution.py:22
  875.9 9.4 copy-start.27
  904.1 7.4 copy-start.18
  919.0 11.3 copy-start.10
  935.2 8.6 copy-start.11
  991.3 30.5 %copy-start.2 = (bf16[4,14,14,12,64]{4,3,2,1,0:T(8,128)(2,1)S(1)}, bf16[4,14,14,12,64]{4,3,2,1,0:T(8,128)(2,1)}, u32[]{:S(2)}) copy-start(bf16[4,14,14,12,64]{4,3,2,1,0:T(8,128)(2,1)} %copy-done.1) | copy-start | bytes 3612676
  1021.8 7.9 copy-start.3
  1021.8 7.9 copy-start.34
  1029.7 3.9 slice-start
  1029.7 3.9 slice-start.1
  1029.7 4.0 copy-start.7
  1029.7 4.0 copy-start.36
  1133.8 13.7 copy-start.29
  1133.8 13.7 copy-start.32
  1133.8 27.6 %collective-permute-start.6 = (bf16[1,29,13,768]{3,1,2,0:T(8,128)(2,1)}, bf16[1,29,13,768]{3,1,2,0:T(8,128)(2,1)}, u32[]{:S(2)}, u32[]{:S(2)}) collective-permute-start(bf16[1,29,13,768]{3,1,2,0:T(8,128)(2,1)} %copy.218), channel_id=1, source_target_pairs={{0,1},{1,2},{2,3},{4,5},{5,6},{6,7},{8,9},{9,10},{10,11},{12,13},{... | collective-permute-start | bytes 1737224 | tf_op jit(solution)/shard_map/ppermute | solution.py:22
  1147.5 3.3 copy-start.37
  1150.8 10.6 copy-start.9
  1161.4 15.5 copy-start.54
  1161.4 18.4 copy-start.51
  1161.4 19.0 %copy-start.52 = (bf16[12,64]{1,0:T(8,128)(2,1)S(1)}, bf16[12,64]{1,0:T(8,128)(2,1)}, u32[]{:S(2)}) copy-start(bf16[12,64]{1,0:T(8,128)(2,1)} %get-tuple-element.168) | copy-start | bytes 4612
  1170.2 18.3 collective-permute-start.7
  1180.5 7.8 copy-start.20
  1180.6 9.0 copy-start.6
  1180.6 9.0 copy-start.39
  1180.6 9.0 copy-start.44
  1180.6 9.3 copy-start.48
  1180.6 9.4 copy-start.42
  1396.1 481.3 %all-reduce.11.cloned.1.call-start = ((), (), s32[]{:S(2)}) async-start(), calls=%async_computation.2 | async-start | bytes 14184448
  (20 other events, 35.4 us)
Sparse Core Ops, SparseCore 0:
  21.3 252.3 all-reduce.6
  1396.2 320.1 all-reduce.8
  1724.7 152.5 all-reduce.10
where the time goes:
time: 1920 us; the launch traced here: 1890 us
  local copies, waits for them, and re-layouts  859 us (45%)
  waiting for transfers between devices  729 us (38%)
  matrix products  155 us (8%)
  other arithmetic  96.1 us (5%)
  between operations  24.1 us (1%)
  starting transfers between devices  22.7 us (1%)
    unnamed x6, waiting for transfers between devices  714 us
    add x8, local copies, waits for them, and re-layouts, scores_of(): direct.reshape(window_count, HEADS, WIN, WIN, WIN, WIN)  297 us
    concatenate x1, local copies, waits for them, and re-layouts, shards(): padded_grad = jnp.concatenate(members)  206 us
    convert_element_type x2, local copies, waits for them, and re-layouts, backward_image(): grad_h = jnp.sum(grid_scores, axis=5, dtype=jnp.float32)  51.6 us
  transfers between devices with their start and end apart: 11, of which 5 were waited for; matrix products, arithmetic and copies ran while one was open for 5% of the time, Pallas kernels for 0%

commit v1 on v0

v1 whole, which is shorter than its diff:
```python
import functools
import math

import jax
import jax.numpy as jnp
from jax import lax
from jax.experimental import pallas as pl
from jax.experimental.pallas import tpu as pltpu
from jax.sharding import PartitionSpec as P

D = 768
HEADS = 12
HEAD_DIM = 64
MLP = 3072
WIN = 14
LANES = 128
CH = D // LANES
PAIRS = HEADS // 2
QROWS = WIN * 16
KROWS = 256
SLOTS = 4
EPS = 1e-06
MESH = pl.DeviceIdType.MESH
F32 = jnp.float32
BF16 = jnp.bfloat16
MIB = 2**20
ANY = pl.BlockSpec(memory_space=pl.ANY)
VM = pl.BlockSpec(memory_space=pltpu.VMEM)

ROW_QKV, ROW_QV, ROW_TBL, ROW_PROJ = 0, 13824, 13836, 13863
ROW_VEC = 18471
ROW_UP, ROW_BUP, ROW_DOWN, ROW_BDOWN, ROW_END = 18501, 36933, 36957, 55389, 55395


def dot(a, b):
    return jnp.dot(a, b, preferred_element_type=F32)


def dot_nt(a, b):
    return lax.dot_general(a, b, (((1,), (1,)), ((), ())), preferred_element_type=F32)


def dot_tn(a, b):
    return lax.dot_general(a, b, (((0,), (0,)), ((), ())), preferred_element_type=F32)


def iota(shape, dim):
    return lax.broadcasted_iota(jnp.int32, shape, dim)


def vmem_params(mib, **more):
    return pltpu.CompilerParams(vmem_limit_bytes=mib * MIB, **more)


def when(cond, fn):
    if cond is None:
        fn()
    else:
        pl.when(cond)(fn)


def coords():
    return lax.axis_index("dp"), lax.axis_index("ty"), lax.axis_index("tx")


def shard_plan(mesh, shard_len):
    count = mesh.shape["dp"] * mesh.shape["ty"] * mesh.shape["tx"]
    rows = -(-(shard_len + LANES - 1) // LANES)
    rows = -(-rows // 32) * 32
    firsts = [shard_len * i // LANES for i in range(count)]
    return count, rows, firsts


def my_flat(mesh):
    d, t, z = coords()
    return (d * mesh.shape["ty"] + t) * mesh.shape["tx"] + z


def prep_kernel(mesh, shard_len, x_ref, o_ref, y_ref):
    rows = x_ref.shape[0]
    shift = lax.rem(lax.rem(my_flat(mesh), 128) * (shard_len % LANES), LANES)
    y_ref[0:8] = jnp.zeros((8, LANES), F32)
    y_ref[8:] = pltpu.roll(x_ref[...], shift, 1)
    keep = iota((rows, LANES), 1) >= shift
    o_ref[...] = jnp.where(keep, y_ref[8:], y_ref[7 : 7 + rows]).astype(BF16)


def prep_params(mesh, params, rows):
    shard_len = params.shape[0]
    padded = jnp.pad(params, (0, rows * LANES - shard_len)).reshape(rows, LANES)
    return pl.pallas_call(
        functools.partial(prep_kernel, mesh, shard_len),
        out_shape=jax.ShapeDtypeStruct((rows, LANES), BF16),
        scratch_shapes=[pltpu.VMEM((rows + 8, LANES), F32)],
        name="prep_params",
        compiler_params=vmem_params(16),
    )(padded)


def finish_kernel(mesh, shard_len, x_ref, o_ref, y_ref):
    rows = x_ref.shape[0]
    shift = lax.rem(lax.rem(my_flat(mesh), 128) * (shard_len % LANES), LANES)
    back = lax.rem(LANES - shift, LANES)
    y_ref[rows:] = jnp.zeros((8, LANES), F32)
    y_ref[:rows] = pltpu.roll(x_ref[...].astype(F32), back, 1)
    keep = iota((rows, LANES), 1) < LANES - shift
    o_ref[...] = jnp.where(keep, y_ref[:rows], y_ref[1 : 1 + rows])


def finish_params(mesh, slab, shard_len):
    rows = slab.shape[0]
    out = pl.pallas_call(
        functools.partial(finish_kernel, mesh, shard_len),
        out_shape=jax.ShapeDtypeStruct((rows, LANES), F32),
        scratch_shapes=[pltpu.VMEM((rows + 8, LANES), F32)],
        name="finish_params",
        compiler_params=vmem_params(16),
    )(slab)
    return out.reshape(-1)[:shard_len]


MATRICES = ((ROW_QKV, D, 3 * D), (ROW_PROJ, D, D), (ROW_UP, D, MLP), (ROW_DOWN, MLP, D))


def table_rows(forward):
    l = iota((128, 32), 0)
    if not forward:
        m = l % 64
        n = jnp.where(m < 27, 27 + m, jnp.where((m >= 32) & (m < 59), m - 32, -1))
        return l // 64, n
    head, n = jnp.zeros_like(l), jnp.full_like(l, -1)
    for h in range(2):
        for base, start in ((13 + 64 * h, 27), (40 + 64 * h, 0)):
            r = (base - l) % 128
            head = jnp.where(r < 27, h, head)
            n = jnp.where(r < 27, start + r, n)
    return head, n


def table_selectors(forward):
    head, n = table_rows(forward)
    hit = (n >= 0) & (iota((128, 32), 1) == n // 2)
    return head, hit & (n % 2 == 0), hit & (n % 2 == 1)


def skewed_table(forward, held):
    head, even, odd = table_selectors(forward)
    head = jnp.concatenate([head] * 4, axis=1)
    e = dot(even.astype(BF16), held)
    o = dot(odd.astype(BF16), held)
    c = iota((128, 128), 1)
    return jnp.where(
        head == c // 64, jnp.where(c < 64, e + pltpu.roll(o, 64, 1), pltpu.roll(e, 64, 1) + o), 0.0
    ).astype(BF16)


def unpack_kernel(firsts, rows, g_ref, *refs):
    outs, vec_ref, tbl_ref = refs[:4], refs[4], refs[5]
    flat = refs[6]
    span = 16
    lead = rows

    def fill(lo, hi):
        for i, first in enumerate(firsts):
            if first + rows <= lo or first >= hi:
                continue
            at = lead + first - lo
            held = flat[at : at + 1]

            def body(k, _):
                flat[pl.ds(at + k * span, span)] = g_ref[
                    i, pl.ds(pl.multiple_of(k * span, span), span)
                ].astype(F32)
                return 0

            lax.fori_loop(0, rows // span, body, 0, unroll=10 if (rows // span) % 10 == 0 else 2)
            if i > 0 and first >= lo:
                flat[at : at + 1] = flat[at : at + 1] + held

    for number, (lo, height, width) in enumerate(MATRICES):
        hi = lo + height * width // LANES
        fill(lo, hi)
        per = width // LANES
        for c in range(per):
            outs[number][:, c * LANES : (c + 1) * LANES] = flat[
                pl.ds(lead + c, height, stride=per), :
            ].astype(BF16)

    vec_ref[...] = jnp.zeros_like(vec_ref)

    def vector(row, at, count, lane):
        for c in range(count):
            vec_ref[row : row + 1, lane + c * LANES : lane + (c + 1) * LANES] = flat[
                at + c : at + c + 1
            ]

    fill(ROW_QV, ROW_PROJ)
    vector(0, lead, 6, 0)
    vector(0, lead + 6, 6, 2 * D)
    held = flat[lead + 12 : lead + 44]
    held = jnp.where(iota((32, LANES), 0) < 27, held, 0.0).astype(BF16)
    tbl_ref[0] = skewed_table(True, held)
    tbl_ref[1] = skewed_table(False, held)
    fill(ROW_VEC, ROW_UP)
    for k in range(5):
        vector(1 + k, lead + 6 * k, 6, 0)
    fill(ROW_BUP, ROW_DOWN)
    vector(6, lead, 24, 0)
    fill(ROW_BDOWN, ROW_END)
    vector(7, lead, 6, 0)


def unpack_params(gathered, firsts):
    count, rows = gathered.shape[:2]
    flat_rows = MLP * D // LANES + 2 * rows + 64
    return pl.pallas_call(
        functools.partial(unpack_kernel, firsts, rows),
        out_shape=[jax.ShapeDtypeStruct((h, w), BF16) for _, h, w in MATRICES]
        + [jax.ShapeDtypeStruct((8, MLP), F32), jax.ShapeDtypeStruct((2, 128, 128), BF16)],
        scratch_shapes=[
            pltpu.VMEM((flat_rows, LANES), F32),
        ],
        name="unpack_params",
        compiler_params=vmem_params(58),
    )(gathered)


PARTS = (("zyx", 1), ("zxy", 1))


def cut_rows(rows):
    tiles, total = rows // 16, sum(share for _, share in PARTS)
    cuts, done, upto_share = [], 0, 0
    for order, share in PARTS:
        upto_share += share
        upto = tiles * upto_share // total
        cuts.append((order, done * 16, (upto - done) * 16))
        done = upto
    return cuts


def relatives(nx, nz):
    every = [
        (rx, ry, rz) for rx in range(nx) for ry in range(2) for rz in range(-(nz - 1), nz)
    ]
    return sorted(every, key=lambda r: r[0] + r[1] + abs(r[2]))


def arrival_axis(order, r):
    axis = None
    for a in order:
        if r["xyz".index(a)] != 0:
            axis = a
    return axis


def forwards(order, r, nx, nz):
    rx, ry, rz = r
    axis, out = arrival_axis(order, r), []
    if axis == "z":
        step = 1 if rz < 0 else -1
        if abs(rz - step) < nz:
            out.append(("z", step, (rx, ry, rz - step)))
    for b in order if axis is None else order[order.index(axis) + 1 :]:
        if b == "x" and nx > 1:
            out.append(("x", 1, (1, ry, rz)))
        if b == "y":
            out.append(("y", 1, (rx, 1, rz)))
        if b == "z":
            out += [("z", 1, (rx, ry, -1)), ("z", -1, (rx, ry, 1))]
    return out


class Place:
    def __init__(self, nx, nz):
        self.nx, self.nz = nx, nz
        self.d, self.t, self.z = coords()
        self.y, self.c = self.t // 2, self.t % 2

    def slab(self, r, core=None):
        c = self.c if core is None else core
        y = self.y if r[1] == 0 else 1 - self.y
        index = (2 * y + c) * self.nz + self.z + r[2]
        if self.nx > 1:
            index = index + (self.d if r[0] == 0 else 1 - self.d) * (4 * self.nz)
        return index

    def exists(self, rz):
        if rz == 0:
            return None
        return (self.z + rz <= self.nz - 1) if rz > 0 else (self.z + rz >= 0)

    def neighbour(self, axis, step):
        if axis == "x":
            return (1 - self.d, self.t, self.z)
        if axis == "y":
            return (self.d, self.t + 2 - 4 * self.y, self.z)
        if axis == "c":
            return (self.d, self.t + 1 - 2 * self.c, self.z)
        return (self.d, self.t, self.z + step)

    def barrier(self):
        sem = pltpu.get_barrier_semaphore()

        def tell(target):
            pl.semaphore_signal(sem, inc=1, device_id=target, device_id_type=MESH)

        tell(self.neighbour("c", 0))
        tell(self.neighbour("y", 0))
        if self.nx > 1:
            tell(self.neighbour("x", 0))
        for step in (-1, 1):
            pl.when(self.exists(step))(lambda step=step: tell(self.neighbour("z", step)))
        inner = (self.z > 0).astype(jnp.int32) + (self.z < self.nz - 1).astype(jnp.int32)
        pl.semaphore_wait(sem, inner + (2 if self.nx == 1 else 3))


def both(a, b):
    if a is None or b is None:
        return b if a is None else a
    return a & b


def gather_kernel(nx, nz, slab_ref, out_ref, send, recv, core_send, core_recv, local_sem):
    rows = slab_ref.shape[0]
    place = Place(nx, nz)
    parts = cut_rows(rows)
    items = relatives(nx, nz)
    own = pltpu.make_async_copy(slab_ref, out_ref.at[place.slab((0, 0, 0))], local_sem)
    own.start()
    place.barrier()
    sends, number = [], 0

    def piece(p, r, core=None):
        _, at, count = parts[p]
        return out_ref.at[place.slab(r, core), pl.ds(at, count)]

    for r in items:
        for p, (order, at, count) in enumerate(parts):
            source = piece(p, r) if r != (0, 0, 0) else slab_ref.at[pl.ds(at, count)]
            there = place.exists(r[2])
            spot = p * len(items) + items.index(r)
            goes = []
            for axis, step, seen in forwards(order, r, nx, nz):
                ok = place.exists(step) if axis == "z" else None
                goes.append(
                    (
                        pltpu.make_async_remote_copy(
                            src_ref=source,
                            dst_ref=piece(p, r),
                            send_sem=send.at[number],
                            recv_sem=recv.at[p * len(items) + items.index(seen)],
                            device_id=place.neighbour(axis, step),
                            device_id_type=MESH,
                        ),
                        both(there, ok),
                    )
                )
                number += 1
            goes.append(
                (
                    pltpu.make_async_remote_copy(
                        src_ref=source,
                        dst_ref=piece(p, r),
                        send_sem=core_send.at[spot],
                        recv_sem=core_recv.at[spot],
                        device_id=place.neighbour("c", 0),
                        device_id_type=MESH,
                    ),
                    there,
                )
            )
            if r != (0, 0, 0):
                arrived = pltpu.make_async_remote_copy(
                    src_ref=source,
                    dst_ref=piece(p, r),
                    send_sem=core_send.at[spot],
                    recv_sem=recv.at[spot],
                    device_id=place.neighbour("c", 0),
                    device_id_type=MESH,
                )
                when(there, arrived.wait_recv)
            for copy, ok in goes:
                when(ok, copy.start)
            sends += goes
    for r in items:
        for p in range(len(parts)):
            spot = p * len(items) + items.index(r)
            arrived = pltpu.make_async_remote_copy(
                src_ref=piece(p, r),
                dst_ref=piece(p, r, 1 - place.c),
                send_sem=core_send.at[spot],
                recv_sem=core_recv.at[spot],
                device_id=place.neighbour("c", 0),
                device_id_type=MESH,
            )
            when(place.exists(r[2]), arrived.wait_recv)
    for copy, ok in sends:
        when(ok, copy.wait_send)
    own.wait()


def count_sends(nx, nz, rows):
    return sum(len(forwards(order, r, nx, nz)) for order, _, _ in cut_rows(rows) for r in relatives(nx, nz))


def gather_params(mesh, slab):
    dp, nz = mesh.shape["dp"], mesh.shape["tx"]
    nx = 2 if dp == 2 else 1
    rows = slab.shape[0]
    if nx == 1:
        slab = lax.all_gather(slab, "dp", axis=0, tiled=True)
    n = len(relatives(nx, nz)) * len(PARTS)
    out = pl.pallas_call(
        functools.partial(gather_kernel, nx, nz),
        out_shape=jax.ShapeDtypeStruct((nx * 4 * nz, slab.shape[0], LANES), BF16),
        in_specs=[ANY],
        out_specs=ANY,
        scratch_shapes=[
            pltpu.SemaphoreType.DMA((count_sends(nx, nz, slab.shape[0]),)),
            pltpu.SemaphoreType.DMA((n,)),
            pltpu.SemaphoreType.DMA((n,)),
            pltpu.SemaphoreType.DMA((n,)),
            pltpu.SemaphoreType.DMA,
        ],
        name="gather_params",
        compiler_params=vmem_params(16, collective_id=4, has_side_effects=True),
    )(slab)
    if nx == 1:
        out = out.reshape(4 * nz, dp, rows, LANES).swapaxes(0, 1).reshape(-1, rows, LANES)
    return out


SEGMENTS = (
    (ROW_QKV, 13824, "qkv", 0),
    (ROW_QV, 39, "attn", 0),
    (ROW_PROJ, 4608, "proj", 0),
    (ROW_VEC, 6, "attn", 40),
    (ROW_VEC + 6, 12, "one", 0),
    (ROW_VEC + 18, 12, "mlp", 0),
    (ROW_UP, 18432, "up", 0),
    (ROW_BUP, 24, "mlp", 16),
    (ROW_DOWN, 18432, "down", 0),
    (ROW_BDOWN, 6, "mlp", 40),
)
BIG = ("qkv", "proj", "up", "down")
SMALL = ("attn", "one", "mlp")


def slab_pieces(first, last):
    out = []
    for start, rows, name, at in SEGMENTS:
        lo, hi = max(first, start), min(last, start + rows)
        if lo < hi:
            out.append((lo - first, hi - lo, name, at + lo - start))
    return out


def block_rows(count):
    tiles = count // 16
    return 16 * max(u for u in range(1, 12) if tiles % u == 0)


def reduce_kernel(nx, nz, dp, shard_len, firsts, rows, *refs):
    big = dict(zip(BIG, refs[:4]))
    small = dict(zip(SMALL, refs[4:7]))
    out_ref = refs[7]
    parts = cut_rows(rows if nx > 1 else rows * dp)
    held, core_in = refs[8], refs[9]
    child_in = refs[10 : 10 + len(parts)]
    stage, whole_slab, total, load_sem, send, recv, core_send, core_recv = refs[10 + len(parts) :]
    place = Place(nx, nz)
    items = relatives(nx, nz)[::-1]
    count = len(firsts)
    group = 4 * nz
    depth = stage.shape[0]
    ends = [min(-(-shard_len * (i + 1) // LANES), ROW_END) for i in range(count)]
    pieces = [slab_pieces(firsts[i], ends[i]) for i in range(count)]

    def loads(i):
        out, at = [], 0
        for _, n, name, row in pieces[i]:
            if name in big:
                lo = row // 8 * 8
                span = -(-(row + n - lo) // 8) * 8
                out.append(
                    pltpu.make_async_copy(
                        big[name].at[pl.ds(lo, span)],
                        stage.at[i % depth, pl.ds(at, span)],
                        load_sem.at[i % depth, len(out)],
                    )
                )
                at += span
        return out

    def target(i):
        return held.at[i % group if nx == 1 else i, pl.ds((i // group) * rows if nx == 1 else 0, rows)]

    step = block_rows(rows)

    def narrow(source, at, dst):
        def body(k, _):
            lo = pl.multiple_of(k * step, 16)
            dst[pl.ds(lo, step)] = source[pl.ds(at + k * step, step)].astype(BF16)
            return 0

        lax.fori_loop(0, rows // step, body, 0)

    def core_copy(j, chip, core):
        return pltpu.make_async_remote_copy(
            src_ref=held.at[j],
            dst_ref=core_in.at[chip],
            send_sem=core_send.at[chip],
            recv_sem=core_recv.at[chip],
            device_id=place.neighbour("c", 0),
            device_id_type=MESH,
        )

    for i in range(min(depth - 1, count)):
        for copy in loads(i):
            copy.start()
    place.barrier()
    for i in range(count):
        if i + depth - 1 < count:
            for copy in loads(i + depth - 1):
                copy.start()
        for copy in loads(i):
            copy.wait()
        if len(pieces[i]) == 1 and pieces[i][0][2] in big:
            narrow(stage.at[i % depth], pieces[i][0][3] % 8, target(i))
        else:
            at = 0
            for dst, n, name, row in pieces[i]:
                if name in big:
                    lo = row // 8 * 8
                    source, src = stage.at[i % depth], at + row - lo
                    at += -(-(row + n - lo) // 8) * 8
                else:
                    source, src = small[name], row
                size = 64
                whole_blocks = n // size
                if whole_blocks:

                    def body(k, _, source=source, src=src, dst=dst, size=size):
                        whole_slab[pl.ds(dst + k * size, size)] = source[pl.ds(src + k * size, size)]
                        return 0

                    lax.fori_loop(0, whole_blocks, body, 0)
                rest = n - whole_blocks * size
                if rest:
                    done = whole_blocks * size
                    whole_slab[dst + done : dst + n] = source[src + done : src + n]
            narrow(whole_slab, 0, target(i))
        if i >= count - group or nx > 1:
            t, z = (i // nz) % 4, i % nz
            chip = (i // group if nx > 1 else 0) * 2 * nz + (t // 2) * nz + z
            pl.when(place.c != t % 2)(core_copy(i if nx > 1 else i % group, chip, 1 - t % 2).start)

    def slots(p):
        order = parts[p][0]
        return [(r, k) for r in items for k in range(len(forwards(order, r, nx, nz)))]

    def chip_of(r):
        y = place.y if r[1] == 0 else 1 - place.y
        index = y * nz + place.z + r[2]
        if nx > 1:
            index = index + (place.d if r[0] == 0 else 1 - place.d) * (2 * nz)
        return index

    base = [0]
    for p in range(len(parts)):
        base.append(base[-1] + len(slots(p)))
    sends, number = [], 0
    for r in items:
        there = place.exists(r[2])
        mine, chip = place.slab(r), chip_of(r)
        when(there, core_copy(mine, chip, place.c).wait_recv)
        for p, (order, at, n) in enumerate(parts):
            children = []
            for k, (axis, move, _) in enumerate(forwards(order, r, nx, nz)):
                slot = slots(p).index((r, k))
                ok = place.exists(move) if axis == "z" else None
                arrived = pltpu.make_async_remote_copy(
                    src_ref=child_in[p].at[slot],
                    dst_ref=child_in[p].at[slot],
                    send_sem=send.at[0],
                    recv_sem=recv.at[base[p] + slot],
                    device_id=place.neighbour("c", 0),
                    device_id_type=MESH,
                )
                when(both(there, ok), arrived.wait_recv)
                children.append((slot, ok))
            block = block_rows(n)
            last = r == (0, 0, 0)

            def add(p=p, at=at, n=n, block=block, children=children, mine=mine, chip=chip, last=last):
                def body(k, _):
                    lo = pl.ds(pl.multiple_of(k * block, 16), block)
                    far = pl.ds(pl.multiple_of(at + k * block, 16), block)
                    acc = held[mine, far].astype(F32) + core_in[chip, far].astype(F32)
                    for slot, ok in children:
                        more = child_in[p][slot, lo].astype(F32)
                        acc = acc + (more if ok is None else jnp.where(ok, more, 0.0))
                    if last:
                        total[far] = acc
                    else:
                        held[mine, far] = acc.astype(BF16)
                    return 0

                lax.fori_loop(0, n // block, body, 0)

            when(there, add)
            if not last:
                axis = arrival_axis(order, r)
                move = 1 if axis != "z" or r[2] > 0 else -1
                up = tuple(
                    v if "xyz"[q] != axis else (v - move if axis == "z" else 0)
                    for q, v in enumerate(r)
                )
                options = forwards(order, up, nx, nz)
                k = [
                    q
                    for q, (b, m, seen) in enumerate(options)
                    if b == axis and seen == r and (b != "z" or m == -move)
                ][0]
                slot = slots(p).index((up, k))
                copy = pltpu.make_async_remote_copy(
                    src_ref=held.at[mine, pl.ds(at, n)],
                    dst_ref=child_in[p].at[slot],
                    send_sem=send.at[number],
                    recv_sem=recv.at[base[p] + slot],
                    device_id=place.neighbour(axis, move),
                    device_id_type=MESH,
                )
                number += 1
                when(there, copy.start)
                sends.append((copy, there))
    for copy, ok in sends:
        when(ok, copy.wait_send)
    for r in items:
        when(place.exists(r[2]), core_copy(place.slab(r, 1 - place.c), chip_of(r), place.c).wait_send)
    if nx > 1:
        me = (place.d * 4 + place.t) * nz + place.z
        shift = lax.rem(lax.rem(me, LANES) * (shard_len % LANES), LANES)
        back = lax.rem(LANES - shift, LANES)
        whole_slab[:rows] = pltpu.roll(total[...], back, 1)
        keep = iota((rows, LANES), 1) < LANES - shift
        out_ref[...] = jnp.where(keep, whole_slab[:rows], whole_slab[1 : 1 + rows])
    else:
        out_ref[...] = total[...].astype(BF16)


def reduce_params(mesh, shard_len, firsts, rows, grads):
    dp, nz = mesh.shape["dp"], mesh.shape["tx"]
    nx = 2 if dp == 2 else 1
    tall = rows if nx > 1 else rows * dp
    items = relatives(nx, nz)
    parts = cut_rows(tall)
    slots = [sum(len(forwards(order, r, nx, nz)) for r in items) for order, _, _ in parts]
    chips = nx * 2 * nz
    out = pl.pallas_call(
        functools.partial(reduce_kernel, nx, nz, dp, shard_len, firsts, rows),
        out_shape=jax.ShapeDtypeStruct((tall, LANES), F32 if nx > 1 else BF16),
        in_specs=[ANY] * 4 + [VM] * 3,
        out_specs=VM,
        scratch_shapes=[
            pltpu.VMEM((nx * 4 * nz, tall, LANES), BF16),
            pltpu.VMEM((chips, tall, LANES), BF16),
        ]
        + [pltpu.VMEM((k, n, LANES), BF16) for k, (_, _, n) in zip(slots, parts)]
        + [
            pltpu.VMEM((4, rows + 32, LANES), F32),
            pltpu.VMEM((rows + 8, LANES), F32),
            pltpu.VMEM((tall, LANES), F32),
            pltpu.SemaphoreType.DMA((4, 2)),
            pltpu.SemaphoreType.DMA((len(items) * len(parts),)),
            pltpu.SemaphoreType.DMA((sum(slots),)),
            pltpu.SemaphoreType.DMA((chips,)),
            pltpu.SemaphoreType.DMA((chips,)),
        ],
        name="reduce_params",
        compiler_params=vmem_params(58, collective_id=5, has_side_effects=True),
    )(*[grads[name] for name in BIG + SMALL])
    if nx > 1:
        return out.reshape(-1)[:shard_len]
    out = lax.psum_scatter(out.reshape(dp, rows, LANES), "dp", scatter_dimension=0, tiled=False)
    return finish_params(mesh, out, shard_len)


HALO_R, HALO_C = 6, 8


def layer_norm_parts(x):
    center = x - jnp.mean(x, axis=-1, keepdims=True)
    inverse = lax.rsqrt(jnp.mean(center * center, axis=-1, keepdims=True) + EPS)
    return center * inverse, inverse


def window_valid(slot, t, z, last_t, last_z):
    ok = None
    if slot // 2 == 1:
        ok = t == last_t
    if slot % 2 == 1:
        ok = (z == last_z) if ok is None else ok & (z == last_z)
    return ok


def halo_exchange(sign, row_src, col_src, row_dst, col_dst, corner_dst, send, recv, limits):
    d, t, z = coords()
    last_t, last_z = limits
    to_t = (t < last_t) if sign > 0 else (t > 0)
    to_z = (z < last_z) if sign > 0 else (z > 0)
    from_t = (t > 0) if sign > 0 else (t < last_t)
    from_z = (z > 0) if sign > 0 else (z < last_z)
    plan = (
        (row_src, row_dst, (d, t + sign, z), to_t, from_t),
        (col_src, col_dst, (d, t, z + sign), to_z, from_z),
        (
            col_src.at[pl.ds(col_src.shape[0] - HALO_R * HALO_C, HALO_R * HALO_C)]
            if sign > 0
            else corner_dst[1],
            corner_dst[0],
            (d, t + sign, z + sign),
            to_t & to_z,
            from_t & from_z,
        ),
    )
    copies = []
    for k, (src, dst, target, sends, receives) in enumerate(plan):
        copy = pltpu.make_async_remote_copy(
            src_ref=src,
            dst_ref=dst,
            send_sem=send.at[k],
            recv_sem=recv.at[k],
            device_id=target,
            device_id_type=MESH,
        )
        pl.when(sends)(copy.start)
        copies.append((copy, sends, receives))

    def wait_recv():
        for copy, _, receives in copies:
            pl.when(receives)(copy.wait_recv)

    def wait_send():
        for copy, sends, _ in copies:
            pl.when(sends)(copy.wait_send)

    return wait_recv, wait_send


def halo_barrier(sign, limits):
    d, t, z = coords()
    last_t, last_z = limits
    sem = pltpu.get_barrier_semaphore()
    to_t = (t < last_t) if sign > 0 else (t > 0)
    to_z = (z < last_z) if sign > 0 else (z > 0)
    from_t = (t > 0) if sign > 0 else (t < last_t)
    from_z = (z > 0) if sign > 0 else (z < last_z)
    for cond, target in (
        (from_t, (d, t - sign, z)),
        (from_z, (d, t, z - sign)),
        (from_t & from_z, (d, t - sign, z - sign)),
    ):
        pl.when(cond)(
            lambda target=target: pl.semaphore_signal(
                sem, inc=1, device_id=target, device_id_type=MESH
            )
        )
    a, b = to_t.astype(jnp.int32), to_z.astype(jnp.int32)
    targets = a + b + a * b
    pl.when(targets > 0)(lambda: pl.semaphore_wait(sem, targets))


def to_windows_kernel(limits, norm, *refs):
    if norm:
        x_ref, vec_ref, w_ref, tile, cols, row_in, col_in, corner_in, ext, send, recv = refs
    else:
        x_ref, w_ref, tile, cols, row_in, col_in, corner_in, ext, send, recv = refs
    d, t, z = coords()
    last_t, last_z = limits
    halo_barrier(1, limits)
    if norm:
        gain, shift = vec_ref[2:3, :D], vec_ref[3:4, :D]
    ext[...] = jnp.zeros_like(ext)
    for r in range(16):
        x = x_ref[pl.ds(r * 16, 16)].astype(F32)
        if norm:
            x = layer_norm_parts(x)[0] * gain + shift
        tile[r] = x.astype(BF16)
        for c in range(CH):
            ext[c, HALO_R + r, 8:24] = x[:, c * LANES : (c + 1) * LANES]
        cols[pl.ds(r * 8, 8)] = x[8:16]
    packed = cols[...].astype(BF16)
    col_in[1] = packed
    wait_recv, wait_send = halo_exchange(
        1,
        tile.at[pl.ds(16 - HALO_R, HALO_R)],
        col_in.at[1],
        row_in,
        col_in.at[0],
        (corner_in,),
        send,
        recv,
        limits,
    )
    wait_recv()

    @pl.when(t > 0)
    def _():
        for r in range(HALO_R):
            x = row_in[r].astype(F32)
            for c in range(CH):
                ext[c, r, 8:24] = x[:, c * LANES : (c + 1) * LANES]

    @pl.when(z > 0)
    def _():
        x = col_in[0].astype(F32)
        for r in range(16):
            for c in range(CH):
                ext[c, HALO_R + r, 0:8] = x[r * 8 : r * 8 + 8, c * LANES : (c + 1) * LANES]

    @pl.when((t > 0) & (z > 0))
    def _():
        x = corner_in[...].astype(F32)
        for r in range(HALO_R):
            for c in range(CH):
                ext[c, r, 0:8] = x[r * 8 : r * 8 + 8, c * LANES : (c + 1) * LANES]

    inside = iota((16, LANES), 0) < WIN
    for slot in range(SLOTS):
        row0 = HALO_R + WIN * (slot // 2) - 2 * t
        col0 = 8 + WIN * (slot % 2) - 2 * z

        def cut(slot=slot, row0=row0, col0=col0):
            for y in range(WIN):
                for c in range(CH):
                    x = ext[c, row0 + y, pl.ds(col0, 16)]
                    w_ref[slot, y * 16 : (y + 1) * 16, c * LANES : (c + 1) * LANES] = jnp.where(
                        inside, x, 0.0
                    ).astype(BF16)

        valid = window_valid(slot, t, z, last_t, last_z)
        if valid is None:
            cut()
        else:
            pl.when(valid)(cut)

            @pl.when(jnp.logical_not(valid))
            def _(slot=slot):
                w_ref[slot] = jnp.zeros((QROWS, D), BF16)

    wait_send()


def halo_scratch():
    return [
        pltpu.VMEM((16, 16, D), BF16),
        pltpu.VMEM((128, D), F32),
        pltpu.VMEM((HALO_R, 16, D), BF16),
        pltpu.VMEM((2, 128, D), BF16),
        pltpu.VMEM((HALO_R * HALO_C, D), BF16),
        pltpu.VMEM((CH, 28, 32, LANES), F32),
        pltpu.SemaphoreType.DMA((3,)),
        pltpu.SemaphoreType.DMA((3,)),
    ]


def to_windows(tokens, vec, limits, collective_id):
    args = (tokens,) if vec is None else (tokens, vec)
    return pl.pallas_call(
        functools.partial(to_windows_kernel, limits, vec is not None),
        out_shape=jax.ShapeDtypeStruct((SLOTS, QROWS, D), BF16),
        in_specs=[VM] * len(args),
        out_specs=VM,
        scratch_shapes=halo_scratch(),
        name="to_windows",
        compiler_params=vmem_params(24, collective_id=collective_id, has_side_effects=True),
    )(*args)


def to_tile_kernel(limits, w_ref, o_ref, tile, cols, row_in, col_in, corner_in, corner_out, ext, send, recv):
    d, t, z = coords()
    last_t, last_z = limits
    halo_barrier(-1, limits)
    for slot in range(SLOTS):
        row0 = HALO_R + WIN * (slot // 2) - 2 * t
        col0 = 8 + WIN * (slot % 2) - 2 * z

        def put(slot=slot, row0=row0, col0=col0):
            for y in range(WIN):
                x = w_ref[slot, y * 16 : (y + 1) * 16].astype(F32)
                for c in range(CH):
                    ext[c, row0 + y, pl.ds(col0, 16)] = x[:, c * LANES : (c + 1) * LANES]

        when(window_valid(slot, t, z, last_t, last_z), put)

    for r in range(HALO_R):
        for c in range(CH):
            tile[r, :, c * LANES : (c + 1) * LANES] = ext[c, r, 8:24].astype(BF16)
            cols[r * 8 : r * 8 + 8, c * LANES : (c + 1) * LANES] = ext[c, r, 0:8]
    corner_out[...] = cols[0 : HALO_R * 8].astype(BF16)
    for r in range(16):
        for c in range(CH):
            cols[r * 8 : r * 8 + 8, c * LANES : (c + 1) * LANES] = ext[c, HALO_R + r, 0:8]
    col_in[1] = cols[...].astype(BF16)
    wait_recv, wait_send = halo_exchange(
        -1,
        tile.at[pl.ds(0, HALO_R)],
        col_in.at[1],
        row_in,
        col_in.at[0],
        (corner_in, corner_out),
        send,
        recv,
        limits,
    )
    wait_recv()
    edge_r, edge_c = WIN - 2 * t, WIN - 2 * z

    @pl.when(t < last_t)
    def _():
        for r in range(HALO_R):

            @pl.when(16 - HALO_R + r >= edge_r)
            def _(r=r):
                x = row_in[r].astype(F32)
                for c in range(CH):
                    ext[c, HALO_R + 16 - HALO_R + r, 8:24] = x[:, c * LANES : (c + 1) * LANES]

    beyond = iota((8, LANES), 0) + 8 >= edge_c

    @pl.when(z < last_z)
    def _():
        x = col_in[0].astype(F32)
        for r in range(16):
            for c in range(CH):
                ext[c, HALO_R + r, 16:24] = jnp.where(
                    beyond,
                    x[r * 8 : r * 8 + 8, c * LANES : (c + 1) * LANES],
                    ext[c, HALO_R + r, 16:24],
                )

    @pl.when((t < last_t) & (z < last_z))
    def _():
        x = corner_in[...].astype(F32)
        for r in range(HALO_R):

            @pl.when(16 - HALO_R + r >= edge_r)
            def _(r=r):
                for c in range(CH):
                    ext[c, 16 + r, 16:24] = jnp.where(
                        beyond,
                        x[r * 8 : r * 8 + 8, c * LANES : (c + 1) * LANES],
                        ext[c, 16 + r, 16:24],
                    )

    for r in range(16):
        for c in range(CH):
            o_ref[r * 16 : (r + 1) * 16, c * LANES : (c + 1) * LANES] = ext[
                c, HALO_R + r, 8:24
            ].astype(BF16)
    wait_send()


def to_tile(windows, limits, collective_id):
    scratch = halo_scratch()
    scratch.insert(5, pltpu.VMEM((HALO_R * HALO_C, D), BF16))
    return pl.pallas_call(
        functools.partial(to_tile_kernel, limits),
        out_shape=jax.ShapeDtypeStruct((256, D), BF16),
        in_specs=[VM],
        out_specs=VM,
        scratch_shapes=scratch,
        name="to_tile",
        compiler_params=vmem_params(24, collective_id=collective_id, has_side_effects=True),
    )(windows)


def fill_one_hots(kp_ref, forward):
    k, l = iota((KROWS, LANES), 0), iota((KROWS, LANES), 1)
    y, x, m = k // 16, k % 16, l % 64
    absent = (x >= WIN) | (y >= WIN)
    if forward:
        hot = ((m < 30) & (m % 16 < WIN) & (m % 16 == x)) | (
            (m >= 32) & (m < 62) & (m % 16 < WIN) & (m % 16 == y)
        )
        value = jnp.where(hot, 1.0, 0.0)
        value = jnp.where(absent, jnp.where(m == 14, -1e30, 0.0), value)
    else:
        hot = ((m < WIN) & (WIN - 1 - m == x)) | ((m >= 32) & (m < 32 + WIN) & (45 - m == y))
        value = jnp.where(hot & jnp.logical_not(absent), 1.0, 0.0)
    for h in range(2):
        kp_ref[h * KROWS : (h + 1) * KROWS, LANES:] = jnp.where(l // 64 == h, value, 0.0).astype(
            BF16
        )
        kp_ref[h * KROWS + QROWS : (h + 1) * KROWS, :LANES] = jnp.zeros((KROWS - QROWS, LANES), BF16)


def head_mask(rows, h):
    return iota((rows, LANES), 1) // 64 == h


def rolled(raw, start):
    by_row = jnp.concatenate(
        [pltpu.roll(raw[y * 16 : (y + 1) * 16], start + y, 1) for y in range(WIN)], axis=0
    )
    by_col = pltpu.roll(raw.reshape(WIN, 16, LANES), 0, 2, stride=1, stride_axis=1)
    return by_row, by_col.reshape(QROWS, LANES)


def skew(raw):
    by_row, by_col = rolled(raw, 5)
    m = iota((QROWS, LANES), 1) % 64
    return jnp.where(m < WIN, by_col, jnp.where((m >= 32) & (m < 32 + WIN), by_row, 0.0))


def unskew(grad):
    by_row, by_col = rolled(grad, 0)
    m = iota((QROWS, LANES), 1) % 64
    return jnp.where(m < 27, by_col, jnp.where((m >= 32) & (m < 59), by_row, 0.0))


def attention_forward(x_ref, w_ref, vec_ref, tbl_ref, qkv_ref, p_ref, a_ref, kp, vs):
    fill_one_hots(kp, True)
    vs[...] = jnp.zeros_like(vs)
    for part in range(3):
        cols = slice(part * D, (part + 1) * D)
        qkv_ref[:, cols] = (dot(x_ref[...], w_ref[:, cols]) + vec_ref[0:1, cols]).astype(BF16)
    lane = iota((QROWS, LANES), 1) % 64
    for p in range(PAIRS):
        q = qkv_ref[:, p * LANES : (p + 1) * LANES]
        k = qkv_ref[:, D + p * LANES : D + (p + 1) * LANES] * jnp.asarray(HEAD_DIM**-0.5, BF16)
        v = qkv_ref[:, 2 * D + p * LANES : 2 * D + (p + 1) * LANES]
        aug = skew(dot_nt(q, tbl_ref[0]))
        high = aug.astype(BF16).astype(F32)
        low = pltpu.roll(aug - high, 16, 1)
        aug = jnp.where(lane == 14, 1.0, high + low).astype(BF16)
        left = jnp.concatenate([q, aug], axis=1)
        zero = jnp.zeros_like(k)
        for h in range(2):
            mask = head_mask(QROWS, h)
            kp[h * KROWS : h * KROWS + QROWS, :LANES] = jnp.where(mask, k, zero)
            vs[h * KROWS : h * KROWS + QROWS] = jnp.where(mask, v, zero)
        for h in range(2):
            s = dot_nt(left, kp[h * KROWS : (h + 1) * KROWS])
            e = jnp.exp(s - jnp.max(s, axis=1, keepdims=True))
            soft = (e / jnp.sum(e, axis=1, keepdims=True)).astype(BF16)
            p_ref[p, :, h * KROWS : (h + 1) * KROWS] = soft
        a_ref[:, p * LANES : (p + 1) * LANES] = dot(p_ref[p], vs[...]).astype(BF16)


def attn_fwd_kernel(valid_ref, x_ref, w_ref, wp_ref, vec_ref, tbl_ref, qkv_ref, p_ref, a_ref, b_ref, kp, vs):
    w = pl.program_id(0)

    @pl.when(valid_ref[w] > 0)
    def _():
        attention_forward(
            x_ref.at[0], w_ref, vec_ref, tbl_ref, qkv_ref.at[0], p_ref.at[0], a_ref.at[0], kp, vs
        )
        b_ref[0] = (dot(a_ref[0], wp_ref[...]) + vec_ref[1:2, :D]).astype(BF16)

    @pl.when(valid_ref[w] == 0)
    def _():
        qkv_ref[...] = jnp.zeros_like(qkv_ref)
        p_ref[...] = jnp.zeros_like(p_ref)
        a_ref[...] = jnp.zeros_like(a_ref)
        b_ref[...] = jnp.zeros_like(b_ref)


def whole(shape):
    return pl.BlockSpec(shape, lambda *_: (0,) * len(shape))


def per_window(shape):
    return pl.BlockSpec((1,) + shape, lambda w, *_: (w,) + (0,) * len(shape))


def attn_fwd(valid, windows, w_qkv, w_proj, vec, tbl):
    return pl.pallas_call(
        attn_fwd_kernel,
        out_shape=[
            jax.ShapeDtypeStruct((SLOTS, QROWS, 3 * D), BF16),
            jax.ShapeDtypeStruct((SLOTS, PAIRS, QROWS, 2 * KROWS), BF16),
            jax.ShapeDtypeStruct((SLOTS, QROWS, D), BF16),
            jax.ShapeDtypeStruct((SLOTS, QROWS, D), BF16),
        ],
        grid_spec=pltpu.PrefetchScalarGridSpec(
            num_scalar_prefetch=1,
            grid=(SLOTS,),
            in_specs=[
                per_window((QROWS, D)),
                whole((D, 3 * D)),
                whole((D, D)),
                whole((8, MLP)),
                whole((2, 128, 128)),
            ],
            out_specs=[
                per_window((QROWS, 3 * D)),
                per_window((PAIRS, QROWS, 2 * KROWS)),
                per_window((QROWS, D)),
                per_window((QROWS, D)),
            ],
            scratch_shapes=[
                pltpu.VMEM((2 * KROWS, 2 * LANES), BF16),
                pltpu.VMEM((2 * KROWS, LANES), BF16),
            ],
        ),
        name="attn_fwd",
        compiler_params=vmem_params(48),
    )(valid, windows, w_qkv, w_proj, vec, tbl)


def attention_backward(ga, qkv_ref, p_ref, tbl_ref, g_ref, gt_ref, kp, vs):
    fill_one_hots(kp, False)
    vs[...] = jnp.zeros_like(vs)
    scale = jnp.asarray(HEAD_DIM**-0.5, BF16)
    for p in range(PAIRS):
        lanes = slice(p * LANES, (p + 1) * LANES)
        q = qkv_ref[:, lanes]
        k = qkv_ref[:, D + p * LANES : D + (p + 1) * LANES] * scale
        v = qkv_ref[:, 2 * D + p * LANES : 2 * D + (p + 1) * LANES]
        da = ga[:, lanes]
        zero = jnp.zeros_like(k)
        for h in range(2):
            mask = head_mask(QROWS, h)
            kp[h * KROWS : h * KROWS + QROWS, :LANES] = jnp.where(mask, k, zero)
            vs[h * KROWS : h * KROWS + QROWS] = jnp.where(mask, v, zero)
        halves = []
        for h in range(2):
            probs = p_ref[p, :, h * KROWS : (h + 1) * KROWS].astype(F32)
            gp = dot_nt(da, vs[h * KROWS : (h + 1) * KROWS])
            both = probs * gp
            inner = jnp.sum(both, axis=1, keepdims=True)
            halves.append((both - probs * inner).astype(BF16))
        ds = jnp.concatenate(halves, axis=1)
        gq = dot(ds, kp[...])
        raw = unskew(gq[:, LANES:]).astype(BF16)
        gt_ref[...] += dot_tn(raw, q)
        g_ref[:, lanes] = (gq[:, :LANES] + dot(raw, tbl_ref[1])).astype(BF16)
        gk = dot_tn(ds, q * scale)
        gv = dot_tn(p_ref[p], da)
        mask = head_mask(QROWS, 0)
        g_ref[:, D + p * LANES : D + (p + 1) * LANES] = jnp.where(
            mask, gk[:QROWS], gk[KROWS : KROWS + QROWS]
        ).astype(BF16)
        g_ref[:, 2 * D + p * LANES : 2 * D + (p + 1) * LANES] = jnp.where(
            mask, gv[:QROWS], gv[KROWS : KROWS + QROWS]
        ).astype(BF16)


def lanes_to_rows(out_ref, row, value):
    for c in range(value.shape[1] // LANES):
        out_ref[row + c : row + c + 1] = value[:, c * LANES : (c + 1) * LANES]


def attn_bwd_kernel(
    valid_ref, gw_ref, x_ref, qkv_ref, p_ref, a_ref, w_ref, wp_ref, tbl_ref,
    gn_ref, gqkv_ref, gproj_ref, small_ref, kp, vs, g_all, gt, ga,
):
    w = pl.program_id(0)

    @pl.when(w == 0)
    def _():
        gt[...] = jnp.zeros_like(gt)

    rows = pl.ds(pl.multiple_of(w * QROWS, 32), QROWS)

    @pl.when(valid_ref[w] > 0)
    def _():
        ga[...] = dot_nt(gw_ref[rows], wp_ref[...]).astype(BF16)
        attention_backward(ga, qkv_ref.at[0], p_ref.at[0], tbl_ref, g_all.at[rows], gt, kp, vs)
        gn_ref[0] = dot_nt(g_all[rows], w_ref[...]).astype(BF16)

    @pl.when(valid_ref[w] == 0)
    def _():
        g_all[rows] = jnp.zeros((QROWS, 3 * D), BF16)
        gn_ref[...] = jnp.zeros_like(gn_ref)

    @pl.when(w == SLOTS - 1)
    def _():
        per = 3 * CH
        for part in range(9):
            cols = slice(part * 256, (part + 1) * 256)
            g = dot_tn(x_ref[...], g_all[:, cols])
            for c in range(2):
                gqkv_ref[pl.ds(part * 2 + c, D, stride=per), :] = g[:, c * LANES : (c + 1) * LANES]
        for part in range(3):
            cols = slice(part * 256, (part + 1) * 256)
            g = dot_tn(a_ref[...], gw_ref[:, cols])
            for c in range(2):
                gproj_ref[pl.ds(part * 2 + c, D, stride=CH), :] = g[:, c * LANES : (c + 1) * LANES]
        small_ref[...] = jnp.zeros_like(small_ref)
        lanes_to_rows(small_ref, 0, jnp.sum(g_all[:, :D].astype(F32), axis=0, keepdims=True))
        lanes_to_rows(small_ref, 6, jnp.sum(g_all[:, 2 * D :].astype(F32), axis=0, keepdims=True))
        lanes_to_rows(small_ref, 40, jnp.sum(gw_ref[...].astype(F32), axis=0, keepdims=True))
        r, c = iota((128, 128), 0), iota((128, 128), 1)
        own = jnp.where(r // 64 == c // 64, gt[...], 0.0)
        own = own + pltpu.roll(own, 64, 1)
        _, even, odd = table_selectors(False)

        def pick(sel):
            return lax.dot_general(
                sel.astype(F32),
                own,
                (((0,), (0,)), ((), ())),
                preferred_element_type=F32,
                precision=lax.Precision.HIGHEST,
            )

        tables = jnp.where(iota((32, LANES), 1) < 64, pick(even), pick(odd))
        small_ref[12:39] = tables[:27]


def attn_bwd(valid, grad_windows, windows, qkv, probs, attended, w_qkv, w_proj, tbl):
    n = SLOTS * QROWS
    return pl.pallas_call(
        attn_bwd_kernel,
        out_shape=[
            jax.ShapeDtypeStruct((SLOTS, QROWS, D), BF16),
            jax.ShapeDtypeStruct((D * 3 * CH, LANES), F32),
            jax.ShapeDtypeStruct((D * CH, LANES), F32),
            jax.ShapeDtypeStruct((48, LANES), F32),
        ],
        grid_spec=pltpu.PrefetchScalarGridSpec(
            num_scalar_prefetch=1,
            grid=(SLOTS,),
            in_specs=[
                whole((n, D)),
                whole((n, D)),
                per_window((QROWS, 3 * D)),
                per_window((PAIRS, QROWS, 2 * KROWS)),
                whole((n, D)),
                whole((D, 3 * D)),
                whole((D, D)),
                whole((2, 128, 128)),
            ],
            out_specs=[
                per_window((QROWS, D)),
                whole((D * 3 * CH, LANES)),
                whole((D * CH, LANES)),
                whole((48, LANES)),
            ],
            scratch_shapes=[
                pltpu.VMEM((2 * KROWS, 2 * LANES), BF16),
                pltpu.VMEM((2 * KROWS, LANES), BF16),
                pltpu.VMEM((n, 3 * D), BF16),
                pltpu.VMEM((128, 128), F32),
                pltpu.VMEM((QROWS, D), BF16),
            ],
        ),
        name="attn_bwd",
        compiler_params=vmem_params(60),
    )(valid, grad_windows.reshape(n, D), windows.reshape(n, D), qkv, probs, attended.reshape(n, D),
      w_qkv, w_proj, tbl)


BLOCK = 512


def mlp_kernel(
    x_ref, br_ref, cot_ref, up_ref, down_ref, vec_ref,
    out_ref, gm_ref, gb_ref, gup_ref, gdown_ref, small_ref,
    hid, xhat, inv, proj, gh, mid,
):
    j = pl.program_id(0)

    @pl.when(j == 0)
    def _():
        middle = x_ref[...].astype(F32) + br_ref[...].astype(F32)
        mid[...] = middle
        normed, inverse = layer_norm_parts(middle)
        xhat[...] = normed
        inv[...] = jnp.broadcast_to(inverse, inv.shape)
        hid[...] = (normed * vec_ref[4:5, :D] + vec_ref[5:6, :D]).astype(BF16)
        proj[...] = jnp.zeros_like(proj)
        gh[...] = jnp.zeros_like(gh)
        small_ref[...] = jnp.zeros_like(small_ref)

    u = dot(hid[...], up_ref[...]) + vec_ref[6:7, pl.ds(pl.multiple_of(j * BLOCK, BLOCK), BLOCK)]
    phi_cum = 0.5 * (1.0 + lax.erf(u * (2.0**-0.5)))
    act = (u * phi_cum).astype(BF16)
    slope = phi_cum + u * (jnp.exp(-0.5 * u * u) * ((2.0 * math.pi) ** -0.5))
    g = dot_nt(cot_ref[...], down_ref[...]) * slope
    gup = g.astype(BF16)
    proj[...] += dot(act, down_ref[...])
    gh[...] += dot_nt(gup, up_ref[...])
    gdown = dot_tn(act, cot_ref[...])
    for c in range(CH):
        gdown_ref[pl.ds(c, BLOCK, stride=CH), :] = gdown[:, c * LANES : (c + 1) * LANES]
    gw = dot_tn(hid[...], gup)
    for c in range(BLOCK // LANES):
        gup_ref[pl.ds(j * (BLOCK // LANES) + c, D, stride=MLP // LANES), :] = gw[:, c * LANES : (c + 1) * LANES]
    gb = jnp.sum(gup.astype(F32), axis=0, keepdims=True)
    for c in range(BLOCK // LANES):
        small_ref[pl.ds(16 + j * (BLOCK // LANES) + c, 1)] = gb[:, c * LANES : (c + 1) * LANES]

    @pl.when(j == pl.num_programs(0) - 1)
    def _():
        down = (proj[...] + vec_ref[7:8, :D]).astype(BF16).astype(F32)
        out_ref[...] = (mid[...] + down).astype(BF16)
        grad = gh[...]
        normed = xhat[...]
        e = grad * vec_ref[4:5, :D]
        cot = cot_ref[...].astype(F32)
        gm = cot + inv[:, :1] * (
            e - jnp.mean(e, axis=1, keepdims=True) - normed * jnp.mean(e * normed, axis=1, keepdims=True)
        )
        gm_ref[...] = gm
        gb_ref[...] = gm.astype(BF16)
        lanes_to_rows(small_ref, 0, jnp.sum(grad * normed, axis=0, keepdims=True))
        lanes_to_rows(small_ref, 6, jnp.sum(grad, axis=0, keepdims=True))
        lanes_to_rows(small_ref, 40, jnp.sum(cot, axis=0, keepdims=True))


def mlp(tokens, branch, cot, w_up, w_down, vec):
    n = tokens.shape[0]
    steps = MLP // BLOCK
    return pl.pallas_call(
        mlp_kernel,
        grid=(steps,),
        out_shape=[
            jax.ShapeDtypeStruct((n, D), BF16),
            jax.ShapeDtypeStruct((n, D), F32),
            jax.ShapeDtypeStruct((n, D), BF16),
            jax.ShapeDtypeStruct((D * MLP // LANES, LANES), F32),
            jax.ShapeDtypeStruct((MLP * CH, LANES), F32),
            jax.ShapeDtypeStruct((48, LANES), F32),
        ],
        in_specs=[
            whole((n, D)),
            whole((n, D)),
            whole((n, D)),
            pl.BlockSpec((D, BLOCK), lambda j: (0, j)),
            pl.BlockSpec((BLOCK, D), lambda j: (j, 0)),
            whole((8, MLP)),
        ],
        out_specs=[
            whole((n, D)),
            whole((n, D)),
            whole((n, D)),
            whole((D * MLP // LANES, LANES)),
            pl.BlockSpec((BLOCK * CH, LANES), lambda j: (j, 0)),
            whole((48, LANES)),
        ],
        scratch_shapes=[
            pltpu.VMEM((n, D), BF16),
            pltpu.VMEM((n, D), F32),
            pltpu.VMEM((n, LANES), F32),
            pltpu.VMEM((n, D), F32),
            pltpu.VMEM((n, D), F32),
            pltpu.VMEM((n, D), F32),
        ],
        name="mlp",
        compiler_params=vmem_params(48),
    )(tokens, branch, cot, w_up, w_down, vec)


def norm_back_kernel(x_ref, gn_ref, gm_ref, vec_ref, o_ref, small_ref):
    normed, inverse = layer_norm_parts(x_ref[...].astype(F32))
    grad = gn_ref[...].astype(F32)
    e = grad * vec_ref[2:3, :D]
    o_ref[...] = (
        gm_ref[...]
        + inverse
        * (e - jnp.mean(e, axis=1, keepdims=True) - normed * jnp.mean(e * normed, axis=1, keepdims=True))
    ).astype(BF16)
    small_ref[...] = jnp.zeros_like(small_ref)
    lanes_to_rows(small_ref, 0, jnp.sum(grad * normed, axis=0, keepdims=True))
    lanes_to_rows(small_ref, 6, jnp.sum(grad, axis=0, keepdims=True))


def norm_back(tokens, grad_normed, grad_middle, vec):
    n = tokens.shape[0]
    return pl.pallas_call(
        norm_back_kernel,
        out_shape=[jax.ShapeDtypeStruct((n, D), BF16), jax.ShapeDtypeStruct((16, LANES), F32)],
        name="norm_back",
        compiler_params=vmem_params(24),
    )(tokens, grad_normed, grad_middle, vec)


def shards(mesh, image_in, params, cotangent):
    axes = ("dp", "ty", "tx")
    shard_len = params.shape[0]
    count, rows, firsts = shard_plan(mesh, shard_len)
    limits = (mesh.shape["ty"] - 1, mesh.shape["tx"] - 1)
    tokens = image_in.reshape(-1, D)
    cot = cotangent.reshape(-1, D)
    t, z = lax.axis_index("ty"), lax.axis_index("tx")
    low, right = (t == limits[0]).astype(jnp.int32), (z == limits[1]).astype(jnp.int32)
    valid = jnp.stack([jnp.int32(1), right, low, low * right])

    slab = prep_params(mesh, params, rows)
    gathered = gather_params(mesh, slab)
    w_qkv, w_proj, w_up, w_down, vec, tbl = unpack_params(gathered, firsts)

    windows = to_windows(tokens, vec, limits, 0)
    qkv, probs, attended, branch_w = attn_fwd(valid, windows, w_qkv, w_proj, vec, tbl)
    branch = to_tile(branch_w, limits, 1)
    out, grad_middle, grad_branch, g_up, g_down, small_mlp = mlp(
        tokens, branch, cot, w_up, w_down, vec
    )
    grad_windows = to_windows(grad_branch, None, limits, 2)
    gn_w, g_qkv, g_proj, small_attn = attn_bwd(
        valid, grad_windows, windows, qkv, probs, attended, w_qkv, w_proj, tbl
    )
    grad_normed = to_tile(gn_w, limits, 3)
    grad_image, small_one = norm_back(tokens, grad_normed, grad_middle, vec)

    grads = dict(
        qkv=g_qkv, proj=g_proj, up=g_up, down=g_down, attn=small_attn, one=small_one, mlp=small_mlp
    )
    grad_params = reduce_params(mesh, shard_len, firsts, rows, grads)
    return out.reshape(image_in.shape), grad_image.reshape(image_in.shape), grad_params


def solution(mesh):
    return jax.shard_map(
        functools.partial(shards, mesh),
        mesh=mesh,
        in_specs=(P("dp", "ty", "tx", None), P(("dp", "ty", "tx")), P("dp", "ty", "tx", None)),
        out_specs=(P("dp", "ty", "tx", None), P("dp", "ty", "tx", None), P(("dp", "ty", "tx"))),
        check_vma=False,
    )
```

time: 1920 us -> 292 us (0.15); the launches traced: 1890 us -> 290 us
  local copies, waits for them, and re-layouts: 859 us -> 15.9 us
  waiting for transfers between devices: 729 us -> 0 us
  Pallas kernels: 0 us -> 273 us
  matrix products: 155 us -> 0 us
  other arithmetic: 96.1 us -> 0.08 us
  between operations: 24.1 us -> 0.79 us
  starting transfers between devices: 22.7 us -> 0 us
    unnamed x6 -> x0, waiting for transfers between devices: 714 us -> none
    add x9 -> x0, local copies, waits for them, and re-layouts: 297 us -> none  [the longest x8 297 us: scores_of(): direct.reshape(window_count, HEADS, WIN, WIN, WIN, WIN)]
    pallas_call x0 -> x12, Pallas kernels: none -> 273 us  [the longest x1 90 us: reduce_params(): pl.pallas_call(functools.partial(reduce_kernel, nx, nz, dp, shard_len, fi...]
    concatenate x1 -> x0, local copies, waits for them, and re-layouts: 206 us -> none  [shards(): padded_grad = jnp.concatenate(members)]
    dot_general x28 -> x0, matrix products: 155 us -> none  [the longest x1 27.4 us: scores_of(): jnp.einsum('nyxhc,nkhc->nhyxk', grid_queries, keyed, preferred_element_ty...]
    convert_element_type x15 -> x0, local copies, waits for them, and re-layouts: 92.5 us -> none  [the longest x2 51.6 us: backward_image(): grad_h = jnp.sum(grid_scores, axis=5, dtype=jnp.float32)]
    reshape x26 -> x1, local copies, waits for them, and re-layouts: 90.8 us -> 1.23 us  [prep_params(): padded = jnp.pad(params, (0, rows * LANES - shard_len)).reshape(rows, LANES)]
    reduce_sum x13 -> x0, other arithmetic: 51.8 us -> none  [the longest x1 30.5 us: backward_image(): grad_h = jnp.sum(grid_scores, axis=5, dtype=jnp.float32)]
  transfers between devices with their start and end apart: 11 -> 0, of which waited for: 5 -> 0; matrix products, arithmetic and copies ran while one was open for 5% -> 0% of each run, Pallas kernels for 0% -> 0%
where the time goes in v1:
time: 292 us; the launch traced here: 290 us
  Pallas kernels  273 us (93%)
  local copies, waits for them, and re-layouts  15.9 us (5%)
    pallas_call x1, Pallas kernels, reduce_params(): pl.pallas_call(functools.partial(reduce_kernel, nx, nz, dp, shard_len, fi...  90 us
    pallas_call x1, Pallas kernels, gather_params(): pl.pallas_call(functools.partial(gather_kernel, nx, nz), out_shape=jax.Sh...  66.6 us
    pallas_call x2, Pallas kernels, to_tile(): pl.pallas_call(functools.partial(to_tile_kernel, limits), out_shape=jax.S...  26.1 us
    pallas_call x1, Pallas kernels, attn_bwd(): pl.pallas_call(attn_bwd_kernel, out_shape=[jax.ShapeDtypeStruct((SLOTS, Q...  23.4 us
    pallas_call x1, Pallas kernels, unpack_params(): pl.pallas_call(functools.partial(unpack_kernel, firsts, rows), out_shape=...  21.4 us
    pallas_call x1, Pallas kernels, mlp(): pl.pallas_call(mlp_kernel, grid=(steps,), out_shape=[jax.ShapeDtypeStruct...  17 us
    pallas_call x2, Pallas kernels, to_windows(): pl.pallas_call(functools.partial(to_windows_kernel, limits, vec is not No...  14.8 us
    unnamed x30, local copies, waits for them, and re-layouts  12.6 us

profile of v1, /device:TPU:0, one launch (start us, length us, event | category | flops | bytes accessed | tf_op | source)
XLA Modules:
  0.0 289.9 jit_solution(17554788502605032543)
XLA Ops:
  0.6 0.1 pad_add_fusion.valid_ref
  0.7 0.0 copy-start.14
  0.7 1.2 pad_bitcast_fusion.x_ref
  2.0 0.4 prep_params.1.slab_ref
  2.4 66.6 %gather_params.1.g_ref = bf16[32,1760,128]{2,1,0:T(8,128)(2,1)S(1)} custom-call(bf16[1760,128]{1,0:T(8,128)(2,1)S(1)} %prep_params.1.slab_ref), custom_call_target="tpu_custom_call" | custom-call | tf_op jit(solution)/shard_map/gather_params/pallas_call | solution.py:414
  69.0 0.0 copy-start
  69.0 5.1 %copy-done = bf16[32,1760,128]{2,1,0:T(8,128)(2,1)} copy-done((bf16[32,1760,128]{2,1,0:T(8,128)(2,1)}, bf16[32,1760,128]{2,1,0:T(8,128)(2,1)S(1)}, u32[]{:S(2)}) %copy-start) | copy-done | bytes 14417944
  74.1 0.0 copy-start.4
  74.1 21.4 %unpack_params.1 = (bf16[768,2304]{1,0:T(8,128)(2,1)}, bf16[768,768]{1,0:T(8,128)(2,1)}, bf16[768,3072]{1,0:T(8,128)(2,1)}, bf16[3072,768]{1,0:T(8,128)(2,1)}, f...) custom-call(bf16[32,1760,128]{2,1,0:T(8,128)(2,1)} %copy-done), custom_call_target="tpu_custom_call" | custom-call | tf_op jit(solution)/shard_map/unpack_params/pallas_call | solution.py:216
  95.5 0.0 copy-done.4
  95.5 0.0 copy-start.5
  95.5 0.9 copy-done.5
  96.4 8.9 %to_windows.2.x_ref = bf16[4,224,768]{2,1,0:T(8,128)(2,1)S(1)} custom-call(bf16[256,768]{1,0:T(8,128)(2,1)S(1)} %bitcast.15, f32[8,3072]{1,0:T(8,128)S(1)} %copy-done.5), custom_call_target="tpu_custom_call" | custom-call | tf_op jit(solution)/shard_map/to_windows/pallas_call | solution.py:871
  105.3 0.0 copy-start.1
  105.3 0.0 copy-done.14
  105.3 0.0 copy-start.3
  105.3 1.8 copy-done.3
  107.1 0.0 copy-start.6
  107.1 0.9 copy-done.6
  108.0 0.0 copy-start.11
  108.0 0.8 copy-done.11
  108.8 0.0 copy-start.7
  108.8 0.0 copy-start.10
  108.8 11.9 %attn_fwd.1 = (bf16[4,224,2304]{2,1,0:T(8,128)(2,1)}, bf16[4,6,224,512]{3,2,1,0:T(8,128)(2,1)}, bf16[4,224,768]{2,1,0:T(8,128)(2,1)S(1)}, bf16[4,224,768]{2,1,0:T(8,128)(2,1)S(1)}) custom-call(s32[4]{0:T(128)S(1)} %pad_add_fusion.valid_ref, bf16[4,224,768]{2,1,0:T(8,128)(2,1)S(1)} %to_windows.2.x_ref, bf16[768,2304]{1,0:T(8,128)(2,1)} %get-tuple-element.26.w_ref, ...), custom_call_target="tpu_custom_call" | custom-call | tf_op jit(solution)/shard_map/attn_fwd/pallas_call | solution.py:1080
  120.7 0.0 copy-start.9
  120.7 9.0 %to_tile.2.br_ref = bf16[256,768]{1,0:T(8,128)(2,1)S(1)} custom-call(bf16[4,224,768]{2,1,0:T(8,128)(2,1)S(1)} %get-tuple-element.29.w_ref), custom_call_target="tpu_custom_call" | custom-call | tf_op jit(solution)/shard_map/to_tile/pallas_call | solution.py:969
  129.7 0.0 copy-done.7
  129.7 0.0 copy-done.10
  129.7 17.0 %mlp.1 = (bf16[256,768]{1,0:T(8,128)(2,1)}, f32[256,768]{1,0:T(8,128)S(1)}, bf16[256,768]{1,0:T(8,128)(2,1)S(1)}, f32[18432,128]{1,0:T(8,128)}, f32[18432,128]{1,0:T(8,128)}, /*index=5*/f32[48,128]{1,0:T(8,128)S(1)}) custom-call(bf16[256,768]{1,0:T(8,128)(2,1)S(1)} %bitcast.16, bf16[256,768]{1,0:T(8,128)(2,1)S(1)} %to_tile.2.br_ref, ...), custom_call_target="tpu_custom_call" | custom-call | tf_op jit(solution)/shard_map/mlp/pallas_call | solution.py:1319
  146.8 0.0 copy-done.1
  146.8 0.0 copy-done.9
  146.8 0.0 copy-start.12
  146.8 6.0 %to_windows.3 = bf16[4,224,768]{2,1,0:T(8,128)(2,1)S(1)} custom-call(bf16[256,768]{1,0:T(8,128)(2,1)S(1)} %get-tuple-element.33.refs_0_), custom_call_target="tpu_custom_call" | custom-call | tf_op jit(solution)/shard_map/to_windows/pallas_call | solution.py:871
  152.8 0.0 copy-done.12
  152.8 0.0 copy-start.2
  152.8 1.1 copy-done.2
  153.9 23.4 %attn_bwd.1 = (bf16[4,224,768]{2,1,0:T(8,128)(2,1)}, f32[13824,128]{1,0:T(8,128)}, f32[4608,128]{1,0:T(8,128)}, f32[48,128]{1,0:T(8,128)}) custom-call(s32[4]{0:T(128)} %copy-done.14, bf16[896,768]{1,0:T(8,128)(2,1)} %bitcast.14, bf16[896,768]{1,0:T(8,128)(2,1)} %bitcast.13, bf16[4,224,2304]{2,1,0:T(8,128)(2,1)} %get-tuple-element.34.qkv_ref, ...), custom_call_target="tpu_custom_call" | custom-call | tf_op jit(solution)/shard_map/attn_bwd/pallas_call | solution.py:1217
  177.3 0.0 copy-start.8
  177.3 1.3 copy-done.8
  178.7 17.1 %to_tile.3.gn_ref = bf16[256,768]{1,0:T(8,128)(2,1)S(1)} custom-call(bf16[4,224,768]{2,1,0:T(8,128)(2,1)S(1)} %copy-done.8), custom_call_target="tpu_custom_call" | custom-call | tf_op jit(solution)/shard_map/to_tile/pallas_call | solution.py:969
  195.8 1.3 norm_back.1
  197.2 0.0 copy-start.13
  197.2 0.6 copy-done.13
  197.8 90.0 %reduce_params.1 = f32[1760,128]{1,0:T(8,128)} custom-call(f32[13824,128]{1,0:T(8,128)} %get-tuple-element.40.refs_0_, f32[4608,128]{1,0:T(8,128)} %get-tuple-element.41.refs_1_, f32[18432,128]{1,0:T(8,128)} %get-tuple-element.42.refs_2_, f32[18432,128]{1,0:T(8,128)} %get-tuple-element.43.refs_3_, f32[48,128]{1,0:T(8,128)} %get-tuple-element.44.refs_4_, ...), custom_call_target="tpu_custom_call" | custom-call | tf_op jit(solution)/shard_map/reduce_params/pallas_call | solution.py:661
  287.8 2.1 slice.4
Async XLA Ops:
  0.7 104.6 %copy-start.14 = (s32[4]{0:T(128)}, s32[4]{0:T(128)S(1)}, u32[]{:S(2)}) copy-start(s32[4]{0:T(128)S(1)} %pad_add_fusion.valid_ref) | copy-start | bytes 52
  69.0 5.1 %copy-start = (bf16[32,1760,128]{2,1,0:T(8,128)(2,1)}, bf16[32,1760,128]{2,1,0:T(8,128)(2,1)S(1)}, u32[]{:S(2)}) copy-start(bf16[32,1760,128]{2,1,0:T(8,128)(2,1)S(1)} %gather_params.1.g_ref) | copy-start | bytes 43253764
  74.1 21.4 %copy-start.4 = (bf16[1,16,16,768]{3,2,1,0:T(8,128)(2,1)S(1)}, bf16[1,16,16,768]{3,2,1,0:T(8,128)(2,1)}, u32[]{:S(2)}) copy-start(bf16[1,16,16,768]{3,2,1,0:T(8,128)(2,1)} %param.3) | copy-start | bytes 1179652
  95.5 0.9 copy-start.5
  105.3 41.5 %copy-start.1 = (bf16[4,224,768]{2,1,0:T(8,128)(2,1)}, bf16[4,224,768]{2,1,0:T(8,128)(2,1)S(1)}, u32[]{:S(2)}) copy-start(bf16[4,224,768]{2,1,0:T(8,128)(2,1)S(1)} %to_windows.2.x_ref) | copy-start | bytes 4128772
  105.3 1.8 copy-start.3
  107.1 0.9 copy-start.6
  108.0 0.8 copy-start.11
  108.8 20.9 %copy-start.7 = (f32[8,3072]{1,0:T(8,128)S(1)}, f32[8,3072]{1,0:T(8,128)}, u32[]{:S(2)}) copy-start(f32[8,3072]{1,0:T(8,128)} %get-tuple-element.25.refs_1_.vec_ref) | copy-start | bytes 294916
  108.8 20.9 %copy-start.10 = (bf16[1,16,16,768]{3,2,1,0:T(8,128)(2,1)S(1)}, bf16[1,16,16,768]{3,2,1,0:T(8,128)(2,1)}, u32[]{:S(2)}) copy-start(bf16[1,16,16,768]{3,2,1,0:T(8,128)(2,1)} %param.5) | copy-start | bytes 1179652
  120.7 26.1 %copy-start.9 = (bf16[4,224,768]{2,1,0:T(8,128)(2,1)}, bf16[4,224,768]{2,1,0:T(8,128)(2,1)S(1)}, u32[]{:S(2)}) copy-start(bf16[4,224,768]{2,1,0:T(8,128)(2,1)S(1)} %get-tuple-element.36) | copy-start | bytes 4128772
  146.8 6.0 %copy-start.12 = (f32[48,128]{1,0:T(8,128)}, f32[48,128]{1,0:T(8,128)S(1)}, u32[]{:S(2)}) copy-start(f32[48,128]{1,0:T(8,128)S(1)} %get-tuple-element.46.refs_6_) | copy-start | bytes 73732
  152.8 1.1 copy-start.2
  177.3 1.3 copy-start.8
  197.2 0.6 copy-start.13
